TPU v7x, 256 devices: a whole 4x4x8 slice. The times are simulated.
256 devices in a mesh: lon: 32 (over y_hi, z, core), batch: 8 (over y_lo, x).
Axes of the slice: x: 4, y: 4 (y_hi: 2, y_lo: 2; y = y_hi * 2 + y_lo), z: 8, core: 2. Of those that a mesh axis runs over, the one named last changes fastest.
Arguments:
- images: bfloat16 [8, 128, 512, 128], P('batch', None, 'lon'), may hold values from -6 to 6
- weights: bfloat16 [4, 9, 128, 128], replicated, may hold values from -0.3125 to 0.3125
- cotangent: bfloat16 [8, 128, 512, 128], P('batch', None, 'lon'), may hold values from -6 to 6
Outputs:
- features: bfloat16 [8, 128, 512, 128], P('batch', None, 'lon')
- image_grads: bfloat16 [8, 128, 512, 128], P('batch', None, 'lon')
- weight_grads: float32 [4, 1152, 128], P(None, 'lon', 'batch')
All inputs are finite; a program needn't handle non-finite values.
Results may differ from a plain program's by a relative error of at most 0.035.
Values may be sent and summed in bfloat16 or wider, within the bound.
A program may use at most 128 MiB of HBM per device.

v0:
```python
import math

import jax
import jax.numpy as jnp
from jax import lax
from jax.sharding import PartitionSpec as P

LAYERS = 4


def with_halo(cells, sides, width):
    for axis, dim in sides:
        count = lax.axis_size(axis)
        head = lax.slice_in_dim(cells, 0, width, axis=dim)
        tail = lax.slice_in_dim(cells, cells.shape[dim] - width, cells.shape[dim], axis=dim)
        cells = jnp.concatenate(
            [
                lax.ppermute(tail, axis, [(i, (i + 1) % count) for i in range(count)]),
                cells,
                lax.ppermute(head, axis, [((i + 1) % count, i) for i in range(count)]),
            ],
            axis=dim,
        )
    return cells


def gather_taps(padded, dilation, columns):
    height = padded.shape[1]
    padded = jnp.pad(padded, ((0, 0), (dilation, dilation), (0, 0), (0, 0)))
    pieces = [
        padded[
            :,
            dilation + vertical * dilation : dilation + vertical * dilation + height,
            dilation + horizontal * dilation : dilation + horizontal * dilation + columns,
        ]
        for vertical in (-1, 0, 1)
        for horizontal in (-1, 0, 1)
    ]
    return jnp.concatenate(pieces, axis=-1)


def slope(pre):
    value = pre.astype(jnp.float32)
    sigma = jax.nn.sigmoid(value)
    return sigma * (1.0 + value * (1.0 - sigma))


def local(images, weights, cotangent):
    channels = weights.shape[-1]
    columns = images.shape[2]
    scale = 1.0 / math.sqrt(
        images.shape[0] * lax.axis_size("batch") * images.shape[1] * columns * lax.axis_size("lon")
    )
    stacked = weights.reshape(LAYERS, 9 * channels, channels)
    flipped = jnp.transpose(weights[:, ::-1], (0, 1, 3, 2)).reshape(LAYERS, 9 * channels, channels)
    layer_inputs = []
    outputs = []
    preacts = []
    current = images
    for number in range(LAYERS):
        dilation = 2**number
        padded = with_halo(current, (("lon", 2),), dilation)
        layer_inputs.append(padded)
        summed = jnp.einsum(
            "bhwk,kc->bhwc",
            gather_taps(padded, dilation, columns),
            stacked[number],
            preferred_element_type=jnp.float32,
        )
        preacts.append(summed.astype(jnp.bfloat16))
        current = jax.nn.silu(summed).astype(jnp.bfloat16)
        outputs.append(current)
    signal = (cotangent.astype(jnp.float32) * slope(preacts[-1])).astype(jnp.bfloat16)
    gradients = [None] * LAYERS
    input_grad = None
    for number in reversed(range(LAYERS)):
        dilation = 2**number
        partial_term = jnp.einsum(
            "bhwk,bhwc->kc",
            gather_taps(layer_inputs[number], dilation, columns),
            signal,
            preferred_element_type=jnp.float32,
        )
        owned = lax.psum_scatter(
            partial_term.astype(jnp.bfloat16), "batch", scatter_dimension=1, tiled=True
        ).astype(jnp.float32)
        owned = lax.psum_scatter(
            owned.astype(jnp.bfloat16), "lon", scatter_dimension=0, tiled=True
        ).astype(jnp.float32)
        gradients[number] = owned * scale
        spread = with_halo(signal, (("lon", 2),), dilation)
        backward = jnp.einsum(
            "bhwk,kc->bhwc",
            gather_taps(spread, dilation, columns),
            flipped[number],
            preferred_element_type=jnp.float32,
        )
        if number > 0:
            signal = (backward * slope(preacts[number - 1])).astype(jnp.bfloat16)
        else:
            input_grad = backward.astype(jnp.bfloat16)
    return (outputs[-1], input_grad, jnp.stack(gradients))


def solution(mesh):
    return jax.shard_map(
        local,
        mesh=mesh,
        in_specs=(P("batch", None, "lon", None), P(), P("batch", None, "lon", None)),
        out_specs=(
            P("batch", None, "lon", None),
            P("batch", None, "lon", None),
            P(None, "lon", "batch"),
        ),
        check_vma=False,
    )
```

profile of v0, /device:TPU:1, one launch (start us, length us, event | category | flops | bytes accessed | tf_op | source)
XLA Modules:
  0.0 490.8 jit_solution(9187125727722515642)
XLA Ops:
  7.2 1.2 copy.23
  8.5 3.1 collective-permute-start
  11.9 2.1 fusion.125
  13.9 1.0 collective-permute-done.1
  16.7 1.4 fusion.22
  19.1 4.8 collective-permute-start.3
  26.7 1.4 fusion.18
  28.6 6.9 %collective-permute-start.5 = (bf16[1,128,4,128]{3,1,2,0:T(8,128)(2,1)S(1)}, bf16[1,128,4,128]{3,1,2,0:T(8,128)(2,1)S(1)}, u32[]{:S(2)}, u32[]{:S(2)}) collective-permute-start(bf16[1,128,4,128]{3,1,2,0:T(8,128)(2,1)S(1)} %get-tuple-element.32), channel_id=1, source_target_pairs={{8,0},{16,8},{24,16},{32,24},{40,32},{48,40},{56,48},{64,56},{72,6... | collective-permute-start | bytes 393224 | tf_op jit(solution)/shard_map/ppermute | solution.py:20
  38.2 1.4 fusion.14
  39.6 1.1 copy-done
  41.0 0.8 fusion.130
  41.8 6.9 %collective-permute-start.7 = (bf16[1,128,8,128]{3,1,2,0:T(8,128)(2,1)}, bf16[1,128,8,128]{3,1,2,0:T(8,128)(2,1)}, u32[]{:S(2)}, u32[]{:S(2)}) collective-permute-start(bf16[1,128,8,128]{3,1,2,0:T(8,128)(2,1)} %get-tuple-element.30), channel_id=1, source_target_pairs={{8,0},{16,8},{24,16},{32,24},{40,32},{48,40},{56,48},{64,56},{72,6... | collective-permute-start | bytes 786440 | tf_op jit(solution)/shard_map/ppermute | solution.py:20
  48.7 0.8 fusion.124
  49.5 1.8 copy.30
  51.3 0.9 copy.33
  52.5 0.9 copy.31
  54.7 1.2 select_maximum_fusion.2
  56.3 1.1 fusion.112
  57.8 1.1 fusion.111
  59.3 1.7 fusion.84
  61.3 1.1 copy.38
  62.4 0.8 fusion.129
  63.3 5.5 %collective-permute-start.9 = (bf16[1,128,8,128]{3,1,2,0:T(8,128)(2,1)}, bf16[1,128,8,128]{3,1,2,0:T(8,128)(2,1)S(1)}, u32[]{:S(2)}, u32[]{:S(2)}) collective-permute-start(bf16[1,128,8,128]{3,1,2,0:T(8,128)(2,1)} %get-tuple-element.28), channel_id=1, source_target_pairs={{8,0},{16,8},{24,16},{32,24},{40,32},{48,40},{56,48},{64,56},{72,6... | collective-permute-start | bytes 786440 | tf_op jit(solution)/shard_map/ppermute | solution.py:20
  68.8 1.6 fusion.36
  72.2 1.6 fusion.69
  73.9 7.8 %collective-permute-start.11 = (bf16[1,128,4,128]{3,1,2,0:T(8,128)(2,1)S(1)}, bf16[1,128,4,128]{3,1,2,0:T(8,128)(2,1)S(1)}, u32[]{:S(2)}, u32[]{:S(2)}) collective-permute-start(bf16[1,128,4,128]{3,1,2,0:T(8,128)(2,1)S(1)} %get-tuple-element.26), channel_id=1, source_target_pairs={{8,0},{16,8},{24,16},{32,24},{40,32},{48,40},{56,48},{64,56},{72,6... | collective-permute-start | bytes 393224 | tf_op jit(solution)/shard_map/ppermute | solution.py:20
  81.7 1.6 fusion.39
  85.0 1.5 fusion.66
  86.6 6.4 %collective-permute-start.13 = (bf16[1,128,2,128]{3,1,2,0:T(8,128)(2,1)S(1)}, bf16[1,128,2,128]{3,1,2,0:T(8,128)(2,1)S(1)}, u32[]{:S(2)}, u32[]{:S(2)}) collective-permute-start(bf16[1,128,2,128]{3,1,2,0:T(8,128)(2,1)S(1)} %get-tuple-element.24), channel_id=1, source_target_pairs={{8,0},{16,8},{24,16},{32,24},{40,32},{48,40},{56,48},{64,56},{72,6... | collective-permute-start | bytes 196616 | tf_op jit(solution)/shard_map/ppermute | solution.py:20
  93.1 1.6 fusion.42
  96.7 1.5 fusion.63
  98.4 5.5 %collective-permute-start.15 = (bf16[1,128,1,128]{3,1,2,0:T(8,128)(2,1)S(1)}, bf16[1,128,1,128]{3,1,2,0:T(8,128)(2,1)S(1)}, u32[]{:S(2)}, u32[]{:S(2)}) collective-permute-start(bf16[1,128,1,128]{3,1,2,0:T(8,128)(2,1)S(1)} %get-tuple-element.22), channel_id=1, source_target_pairs={{8,0},{16,8},{24,16},{32,24},{40,32},{48,40},{56,48},{64,56},{72,6... | collective-permute-start | bytes 98312 | tf_op jit(solution)/shard_map/ppermute | solution.py:20
  103.8 1.6 fusion.45
  105.8 0.9 slice_dynamic-update-slice_fusion.5
  106.7 0.9 slice_dynamic-update-slice_fusion.4
  107.6 0.9 slice_dynamic-update-slice_fusion.3
  108.5 0.9 fusion.104
  109.4 0.9 constant_dynamic-update-slice_fusion.7
  110.3 0.9 fusion.103
  111.2 1.0 slice_dynamic-update-slice_fusion.2
  112.2 1.0 slice_dynamic-update-slice_fusion.1
  113.2 1.1 slice_dynamic-update-slice_fusion
  114.3 31.2 %reduce-scatter.13.cloned.1.call-done = bf16[1152,16]{0,1:T(8,128)(2,1)} async-done(((bf16[1152,128]{0,1:T(8,128)(2,1)}), bf16[1152,16]{0,1:T(8,128)(2,1)}) %reduce-scatter.13.cloned.1.call-update) | async-done | bytes 36880 | tf_op jit(solution)/shard_map/reduce_scatter | solution.py:84
  145.5 41.3 %reduce-scatter.11.cloned.1.call-done = bf16[1152,16]{0,1:T(8,128)(2,1)} async-done(((bf16[1152,128]{0,1:T(8,128)(2,1)}), bf16[1152,16]{0,1:T(8,128)(2,1)}) %reduce-scatter.11.cloned.1.call-update) | async-done | bytes 36880 | tf_op jit(solution)/shard_map/reduce_scatter | solution.py:84
  186.7 41.3 %reduce-scatter.9.cloned.1.call-done = bf16[1152,16]{0,1:T(8,128)(2,1)} async-done(((bf16[1152,128]{0,1:T(8,128)(2,1)}), bf16[1152,16]{0,1:T(8,128)(2,1)}) %reduce-scatter.9.cloned.1.call-update) | async-done | bytes 36880 | tf_op jit(solution)/shard_map/reduce_scatter | solution.py:84
  228.1 3.7 fusion.73
  231.8 1.1 copy.39
  232.9 248.9 %all-reduce.15.cloned.1.call-done = (bf16[1152,16]{0,1:T(8,128)(2,1)}, bf16[1152,16]{0,1:T(8,128)(2,1)}, bf16[1152,16]{0,1:T(8,128)(2,1)}, bf16[1152,16]{0,1:T(8,128)(2,1)}) async-done(((bf16[1152,16]{0,1:T(8,128)(2,1)}, bf16[1152,16]{0,1:T(8,128)(2,1)}, bf16[1152,16]{0,1:T(8,128)(2,1)}, bf16[1152,16]{0,1:T(8,128)(2,1)}), (bf16[1152,16]{0,1:T(8,128)(2,1)}, bf16[1152,16]{0,1:T(8,128)(2,1)}, ...) | async-done | bytes 147472
  (160 shorter events, 19.2 us)
Async XLA Ops:
  7.2 8.5 %copy-start.7 = (bf16[1,128,16,128]{3,2,1,0:T(8,128)(2,1)S(1)}, bf16[1,128,16,128]{3,2,1,0:T(8,128)(2,1)}, u32[]{:S(2)}) copy-start(bf16[1,128,16,128]{3,2,1,0:T(8,128)(2,1)} %param.3) | copy-start | bytes 1572868
  7.2 107.1 %reduce-scatter.15.cloned.1.call-start = ((), (), s32[]{:S(2)}) async-start(), calls=%async_computation.7 | async-start | bytes 331776 | tf_op jit(solution)/shard_map/reduce_scatter | solution.py:84
  8.5 5.5 %collective-permute-start = (bf16[1,128,1,128]{3,1,2,0:T(8,128)(2,1)S(1)}, bf16[1,128,1,128]{3,1,2,0:T(8,128)(2,1)S(1)}, u32[]{:S(2)}, u32[]{:S(2)}) collective-permute-start(bf16[1,128,1,128]{3,1,2,0:T(8,128)(2,1)S(1)} %get-tuple-element.35), channel_id=1, source_target_pairs={{0,8},{8,16},{16,24},{24,32},{32,40},{40,48},{48,56},{56,64},{64,7... | collective-permute-start | bytes 98312 | tf_op jit(solution)/shard_map/ppermute | solution.py:18
  11.6 3.3 collective-permute-start.1
  16.7 8.4 %copy-start.3 = (bf16[1,128,16,1152]{3,1,2,0:T(8,128)(2,1)}, bf16[1,128,16,1152]{3,1,2,0:T(8,128)(2,1)S(1)}, u32[]{:S(2)}) copy-start(bf16[1,128,16,1152]{3,1,2,0:T(8,128)(2,1)S(1)} %slice_dynamic-update-slice_fusion.42) | copy-start | bytes 14155780
  18.5 6.1 %collective-permute-start.2 = (bf16[1,128,2,128]{3,1,2,0:T(8,128)(2,1)S(1)}, bf16[1,128,2,128]{3,1,2,0:T(8,128)(2,1)S(1)}, u32[]{:S(2)}, u32[]{:S(2)}) collective-permute-start(bf16[1,128,2,128]{3,1,2,0:T(8,128)(2,1)S(1)} %get-tuple-element.33), channel_id=1, source_target_pairs={{0,8},{8,16},{16,24},{24,32},{32,40},{40,48},{48,56},{56,64},{64,7... | collective-permute-start | bytes 196616 | tf_op jit(solution)/shard_map/ppermute | solution.py:18
  19.1 5.7 %collective-permute-start.3 = (bf16[1,128,2,128]{3,1,2,0:T(8,128)(2,1)S(1)}, bf16[1,128,2,128]{3,1,2,0:T(8,128)(2,1)S(1)}, u32[]{:S(2)}, u32[]{:S(2)}) collective-permute-start(bf16[1,128,2,128]{3,1,2,0:T(8,128)(2,1)S(1)} %get-tuple-element.34), channel_id=1, source_target_pairs={{8,0},{16,8},{24,16},{32,24},{40,32},{48,40},{56,48},{64,56},{72,6... | collective-permute-start | bytes 196616 | tf_op jit(solution)/shard_map/ppermute | solution.py:20
  26.5 8.9 %copy-start.6 = (bf16[4,9,128,128]{3,2,1,0:T(8,128)(2,1)S(1)}, bf16[4,9,128,128]{3,2,1,0:T(8,128)(2,1)}, u32[]{:S(2)}) copy-start(bf16[4,9,128,128]{3,2,1,0:T(8,128)(2,1)} %param.4) | copy-start | bytes 3538948
  26.7 8.8 %copy-start.4 = (bf16[1,128,16,1152]{3,1,2,0:T(8,128)(2,1)}, bf16[1,128,16,1152]{3,1,2,0:T(8,128)(2,1)S(1)}, u32[]{:S(2)}) copy-start(bf16[1,128,16,1152]{3,1,2,0:T(8,128)(2,1)S(1)} %slice_dynamic-update-slice_fusion.36) | copy-start | bytes 14155780
  28.5 7.2 %collective-permute-start.4 = (bf16[1,128,4,128]{3,1,2,0:T(8,128)(2,1)S(1)}, bf16[1,128,4,128]{3,1,2,0:T(8,128)(2,1)S(1)}, u32[]{:S(2)}, u32[]{:S(2)}) collective-permute-start(bf16[1,128,4,128]{3,1,2,0:T(8,128)(2,1)S(1)} %get-tuple-element.31), channel_id=1, source_target_pairs={{0,8},{8,16},{16,24},{24,32},{32,40},{40,48},{48,56},{56,64},{64,7... | collective-permute-start | bytes 393224 | tf_op jit(solution)/shard_map/ppermute | solution.py:18
  28.6 7.8 %collective-permute-start.5 = (bf16[1,128,4,128]{3,1,2,0:T(8,128)(2,1)S(1)}, bf16[1,128,4,128]{3,1,2,0:T(8,128)(2,1)S(1)}, u32[]{:S(2)}, u32[]{:S(2)}) collective-permute-start(bf16[1,128,4,128]{3,1,2,0:T(8,128)(2,1)S(1)} %get-tuple-element.32), channel_id=1, source_target_pairs={{8,0},{16,8},{24,16},{32,24},{40,32},{48,40},{56,48},{64,56},{72,6... | collective-permute-start | bytes 393224 | tf_op jit(solution)/shard_map/ppermute | solution.py:20
  38.2 11.3 %copy-start.5 = (bf16[1,128,16,1152]{3,1,2,0:T(8,128)(2,1)}, bf16[1,128,16,1152]{3,1,2,0:T(8,128)(2,1)S(1)}, u32[]{:S(2)}) copy-start(bf16[1,128,16,1152]{3,1,2,0:T(8,128)(2,1)S(1)} %slice_dynamic-update-slice_fusion.30) | copy-start | bytes 14155780
  39.6 1.1 copy-start
  40.7 12.7 %copy-start.13 = (u32[256]{0:T(256)S(1)}, u32[256]{0:T(256)}, u32[]{:S(2)}) copy-start(u32[256]{0:T(256)} %constant.32) | copy-start | bytes 3076
  41.8 12.8 %collective-permute-start.6 = (bf16[1,128,8,128]{3,1,2,0:T(8,128)(2,1)}, bf16[1,128,8,128]{3,1,2,0:T(8,128)(2,1)}, u32[]{:S(2)}, u32[]{:S(2)}) collective-permute-start(bf16[1,128,8,128]{3,1,2,0:T(8,128)(2,1)} %get-tuple-element.29), channel_id=1, source_target_pairs={{0,8},{8,16},{16,24},{24,32},{32,40},{40,48},{48,56},{56,64},{64,7... | collective-permute-start | bytes 786440 | tf_op jit(solution)/shard_map/ppermute | solution.py:18
  41.8 12.8 %collective-permute-start.7 = (bf16[1,128,8,128]{3,1,2,0:T(8,128)(2,1)}, bf16[1,128,8,128]{3,1,2,0:T(8,128)(2,1)}, u32[]{:S(2)}, u32[]{:S(2)}) collective-permute-start(bf16[1,128,8,128]{3,1,2,0:T(8,128)(2,1)} %get-tuple-element.30), channel_id=1, source_target_pairs={{8,0},{16,8},{24,16},{32,24},{40,32},{48,40},{56,48},{64,56},{72,6... | collective-permute-start | bytes 786440 | tf_op jit(solution)/shard_map/ppermute | solution.py:20
  54.6 2.8 copy-start.1
  56.0 3.3 copy-start.9
  56.0 3.3 copy-start.12
  63.3 7.4 %collective-permute-start.8 = (bf16[1,128,8,128]{3,1,2,0:T(8,128)(2,1)}, bf16[1,128,8,128]{3,1,2,0:T(8,128)(2,1)S(1)}, u32[]{:S(2)}, u32[]{:S(2)}) collective-permute-start(bf16[1,128,8,128]{3,1,2,0:T(8,128)(2,1)} %get-tuple-element.27), channel_id=1, source_target_pairs={{0,8},{8,16},{16,24},{24,32},{32,40},{40,48},{48,56},{56,64},{64,7... | collective-permute-start | bytes 786440 | tf_op jit(solution)/shard_map/ppermute | solution.py:18
  63.3 7.4 %collective-permute-start.9 = (bf16[1,128,8,128]{3,1,2,0:T(8,128)(2,1)}, bf16[1,128,8,128]{3,1,2,0:T(8,128)(2,1)S(1)}, u32[]{:S(2)}, u32[]{:S(2)}) collective-permute-start(bf16[1,128,8,128]{3,1,2,0:T(8,128)(2,1)} %get-tuple-element.28), channel_id=1, source_target_pairs={{8,0},{16,8},{24,16},{32,24},{40,32},{48,40},{56,48},{64,56},{72,6... | collective-permute-start | bytes 786440 | tf_op jit(solution)/shard_map/ppermute | solution.py:20
  70.4 75.1 %reduce-scatter.13.cloned.1.call-start = ((), (), s32[]{:S(2)}) async-start(), calls=%async_computation.6 | async-start | bytes 331776 | tf_op jit(solution)/shard_map/reduce_scatter | solution.py:84
  70.9 1.2 copy-start.2
  70.9 1.3 copy-start.11
  71.9 9.8 %slice-start.4 = ((s8[4718592]{0:T(1024)(128)(4,1)}), s8[4194304]{0:T(1024)(128)(4,1)S(1)}, s32[]{:S(2)}) async-start(s8[4718592]{0:T(1024)(128)(4,1)} %bitcast.183), calls=%async_computation.13 | async-start | bytes 8388608
  72.2 9.5 %slice-start.5 = ((s8[4718592]{0:T(1024)(128)(4,1)}), s8[524288]{0:T(1024)(128)(4,1)S(1)}, s32[]{:S(2)}) async-start(s8[4718592]{0:T(1024)(128)(4,1)} %bitcast.183), calls=%async_computation.14 | async-start | bytes 1048576
  73.8 9.6 %collective-permute-start.10 = (bf16[1,128,4,128]{3,1,2,0:T(8,128)(2,1)S(1)}, bf16[1,128,4,128]{3,1,2,0:T(8,128)(2,1)S(1)}, u32[]{:S(2)}, u32[]{:S(2)}) collective-permute-start(bf16[1,128,4,128]{3,1,2,0:T(8,128)(2,1)S(1)} %get-tuple-element.25), channel_id=1, source_target_pairs={{0,8},{8,16},{16,24},{24,32},{32,40},{40,48},{48,56},{56,64},{64,7... | collective-permute-start | bytes 393224 | tf_op jit(solution)/shard_map/ppermute | solution.py:18
  73.9 9.5 %collective-permute-start.11 = (bf16[1,128,4,128]{3,1,2,0:T(8,128)(2,1)S(1)}, bf16[1,128,4,128]{3,1,2,0:T(8,128)(2,1)S(1)}, u32[]{:S(2)}, u32[]{:S(2)}) collective-permute-start(bf16[1,128,4,128]{3,1,2,0:T(8,128)(2,1)S(1)} %get-tuple-element.26), channel_id=1, source_target_pairs={{8,0},{16,8},{24,16},{32,24},{40,32},{48,40},{56,48},{64,56},{72,6... | collective-permute-start | bytes 393224 | tf_op jit(solution)/shard_map/ppermute | solution.py:20
  83.3 103.4 %reduce-scatter.11.cloned.1.call-start = ((), (), s32[]{:S(2)}) async-start(), calls=%async_computation.5 | async-start | bytes 331776 | tf_op jit(solution)/shard_map/reduce_scatter | solution.py:84
  83.7 1.3 copy-start.10
  84.7 8.4 %slice-start.2 = ((s8[4718592]{0:T(1024)(128)(4,1)}), s8[4194304]{0:T(1024)(128)(4,1)S(1)}, s32[]{:S(2)}) async-start(s8[4718592]{0:T(1024)(128)(4,1)} %bitcast.181), calls=%async_computation.11 | async-start | bytes 8388608
  85.0 8.1 %slice-start.3 = ((s8[4718592]{0:T(1024)(128)(4,1)}), s8[524288]{0:T(1024)(128)(4,1)S(1)}, s32[]{:S(2)}) async-start(s8[4718592]{0:T(1024)(128)(4,1)} %bitcast.181), calls=%async_computation.12 | async-start | bytes 1048576
  86.5 8.4 %collective-permute-start.12 = (bf16[1,128,2,128]{3,1,2,0:T(8,128)(2,1)S(1)}, bf16[1,128,2,128]{3,1,2,0:T(8,128)(2,1)S(1)}, u32[]{:S(2)}, u32[]{:S(2)}) collective-permute-start(bf16[1,128,2,128]{3,1,2,0:T(8,128)(2,1)S(1)} %get-tuple-element.23), channel_id=1, source_target_pairs={{0,8},{8,16},{16,24},{24,32},{32,40},{40,48},{48,56},{56,64},{64,7... | collective-permute-start | bytes 196616 | tf_op jit(solution)/shard_map/ppermute | solution.py:18
  86.6 8.4 %collective-permute-start.13 = (bf16[1,128,2,128]{3,1,2,0:T(8,128)(2,1)S(1)}, bf16[1,128,2,128]{3,1,2,0:T(8,128)(2,1)S(1)}, u32[]{:S(2)}, u32[]{:S(2)}) collective-permute-start(bf16[1,128,2,128]{3,1,2,0:T(8,128)(2,1)S(1)} %get-tuple-element.24), channel_id=1, source_target_pairs={{8,0},{16,8},{24,16},{32,24},{40,32},{48,40},{56,48},{64,56},{72,6... | collective-permute-start | bytes 196616 | tf_op jit(solution)/shard_map/ppermute | solution.py:20
  94.7 133.3 %reduce-scatter.9.cloned.1.call-start = ((), (), s32[]{:S(2)}) async-start(), calls=%async_computation.4 | async-start | bytes 331776 | tf_op jit(solution)/shard_map/reduce_scatter | solution.py:84
  96.3 7.6 %slice-start = ((s8[4718592]{0:T(1024)(128)(4,1)}), s8[4194304]{0:T(1024)(128)(4,1)S(1)}, s32[]{:S(2)}) async-start(s8[4718592]{0:T(1024)(128)(4,1)} %bitcast.179), calls=%async_computation.9 | async-start | bytes 8388608
  96.7 7.1 %slice-start.1 = ((s8[4718592]{0:T(1024)(128)(4,1)}), s8[524288]{0:T(1024)(128)(4,1)S(1)}, s32[]{:S(2)}) async-start(s8[4718592]{0:T(1024)(128)(4,1)} %bitcast.179), calls=%async_computation.10 | async-start | bytes 1048576
  98.3 7.3 %collective-permute-start.14 = (bf16[1,128,1,128]{3,1,2,0:T(8,128)(2,1)S(1)}, bf16[1,128,1,128]{3,1,2,0:T(8,128)(2,1)S(1)}, u32[]{:S(2)}, u32[]{:S(2)}) collective-permute-start(bf16[1,128,1,128]{3,1,2,0:T(8,128)(2,1)S(1)} %get-tuple-element.21), channel_id=1, source_target_pairs={{0,8},{8,16},{16,24},{24,32},{32,40},{40,48},{48,56},{56,64},{64,7... | collective-permute-start | bytes 98312 | tf_op jit(solution)/shard_map/ppermute | solution.py:18
  98.4 7.2 %collective-permute-start.15 = (bf16[1,128,1,128]{3,1,2,0:T(8,128)(2,1)S(1)}, bf16[1,128,1,128]{3,1,2,0:T(8,128)(2,1)S(1)}, u32[]{:S(2)}, u32[]{:S(2)}) collective-permute-start(bf16[1,128,1,128]{3,1,2,0:T(8,128)(2,1)S(1)} %get-tuple-element.22), channel_id=1, source_target_pairs={{8,0},{16,8},{24,16},{32,24},{40,32},{48,40},{56,48},{64,56},{72,6... | collective-permute-start | bytes 98312 | tf_op jit(solution)/shard_map/ppermute | solution.py:20
  105.5 376.3 %all-reduce.15.cloned.1.call-start = ((), (), s32[]{:S(2)}) async-start(), calls=%async_computation.8 | async-start | bytes 294912
  105.8 122.3 %copy-start.8 = (bf16[1,9,128,128]{3,2,1,0:T(8,128)(2,1)S(1)}, bf16[1,9,128,128]{3,2,1,0:T(8,128)(2,1)}, u32[]{:S(2)}) copy-start(bf16[1,9,128,128]{3,2,1,0:T(8,128)(2,1)} %copy.33) | copy-start | bytes 884740
Sparse Core Ops, SparseCore 0:
  70.5 33.7 reduce-scatter.14
  107.0 38.3 reduce-scatter.12
  148.0 38.6 reduce-scatter.10
  189.2 38.7 reduce-scatter.8
  230.7 251.0 all-reduce.14
where the time goes:
time: 499 us; the launch traced here: 491 us
  waiting for transfers between devices  365 us (73%)
  starting transfers between devices  48.6 us (10%)
  local copies, waits for them, and re-layouts  27.8 us (6%)
  matrix products  20.8 us (4%)
  between operations  15.7 us (3%)
  other arithmetic  12.4 us (2%)
    unnamed x6, waiting for transfers between devices  249 us
    reduce_scatter x4, waiting for transfers between devices, local(): lax.psum_scatter(partial_term.astype(jnp.bfloat16), 'batch', scatter_dime...  114 us
    ppermute x8, starting transfers between devices, with_halo(): lax.ppermute(head, axis, [((i + 1) % count, i) for i in range(count)])  44.1 us
    unnamed x89, local copies, waits for them, and re-layouts  16.9 us
  transfers between devices with their start and end apart: 21, of which 9 were waited for; matrix products, arithmetic and copies ran while one was open for 7% of the time, Pallas kernels for 0%

commit v1 on v0

v1 whole, which is shorter than its diff:
```python
import functools
import math

import jax
import jax.numpy as jnp
from jax import lax
from jax.experimental import pallas as pl
from jax.experimental.pallas import tpu as pltpu
from jax.sharding import PartitionSpec as P

LAYERS = 4
PAD = 8
BF16 = jnp.bfloat16
F32 = jnp.float32
MESH = pl.DeviceIdType.MESH


def swapped(value):
    return jnp.swapaxes(value, 0, 1)


def kernel(
    ring, images_ref, weights_ref, cotangent_ref, features_ref, input_grad_ref, owned_ref, *scratch
):
    groups, ranks = ring
    (staged, upstream, columns_up, taps, forward_w, backward_w, shifter, slabs, out_a, out_b) = scratch[:10]
    levels = scratch[10:14]
    signals = scratch[14:18]
    slopes = scratch[18]
    send_b, recv_b, send_l, recv_l, local_sem = scratch[19:24]
    halo_send, halo_recv, batch_send, batch_recv, lon_send, lon_recv = scratch[24:30]

    lon = lax.axis_index("lon")
    batch = lax.axis_index("batch")
    right, left = lax.rem(lon + 1, groups), lax.rem(lon + groups - 1, groups)
    rows, width, channels = staged.shape

    fetch_images = pltpu.make_async_copy(images_ref, staged, local_sem.at[0])
    fetch_taps = pltpu.make_async_copy(weights_ref, taps, local_sem.at[1])
    fetch_upstream = pltpu.make_async_copy(cotangent_ref, upstream, local_sem.at[2])
    fetch_images.start()
    fetch_taps.start()
    fetch_upstream.start()

    barrier = pltpu.get_barrier_semaphore()

    @pl.loop(1, groups)
    def _(step):
        pl.semaphore_signal(
            barrier, inc=1, device_id={"lon": lax.rem(lon + step, groups)}, device_id_type=MESH
        )

    @pl.loop(1, ranks)
    def _(step):
        pl.semaphore_signal(
            barrier, inc=1, device_id={"batch": lax.rem(batch + step, ranks)}, device_id_type=MESH
        )

    def halo_copy(kind, number, side, place):
        dilation = 2**number
        buffer = (levels, signals)[kind][number]
        source = width + place if side == 0 else dilation + place
        target = place if side == 0 else dilation + width + place
        return pltpu.make_async_remote_copy(
            src_ref=buffer.at[1, source],
            dst_ref=buffer.at[1, target],
            send_sem=halo_send.at[kind, number, side, place],
            recv_sem=halo_recv.at[kind, number, side, place],
            device_id={"lon": right if side == 0 else left},
            device_id_type=MESH,
        )

    def send_column(kind, number, column):
        dilation = 2**number
        if column < dilation:
            halo_copy(kind, number, 1, column).start()
        if column >= width - dilation:
            halo_copy(kind, number, 0, column - (width - dilation)).start()

    def fill(buffer, dilation, slot, value):
        shifter[slot, pl.ds(PAD, rows), :] = value
        buffer[0, slot] = shifter[slot, pl.ds(PAD - dilation, rows), :].astype(BF16)
        buffer[2, slot] = shifter[slot, pl.ds(PAD + dilation, rows), :].astype(BF16)

    def receive(kind, number, side, place):
        dilation = 2**number
        buffer = (levels, signals)[kind][number]
        halo_copy(kind, number, side, place).wait_recv()
        slot = place if side == 0 else dilation + width + place
        fill(buffer, dilation, slot, buffer[1, slot].astype(F32))

    def build_forward(number):
        for span in range(4):
            for row in range(3):
                for side in range(2):
                    column = span - side
                    block = (
                        taps[number, 3 * row + column]
                        if 0 <= column < 3
                        else jnp.zeros((channels, channels), BF16)
                    )
                    forward_w[
                        number,
                        pl.ds((3 * span + row) * channels, channels),
                        pl.ds(side * channels, channels),
                    ] = block

    def build_backward(number):
        for span in range(4):
            for row in range(3):
                for side in range(2):
                    column = span - side
                    block = (
                        taps[number, 8 - (3 * row + column)]
                        if 0 <= column < 3
                        else jnp.zeros((channels, channels), BF16)
                    )
                    backward_w[
                        number,
                        pl.ds(side * channels, channels),
                        pl.ds((3 * span + row) * channels, channels),
                    ] = block

    def gathered(buffer, dilation, column):
        return jnp.concatenate(
            [buffer[row, column + span * dilation] for span in range(4) for row in range(3)], axis=-1
        )

    def pairs_of(dilation):
        firsts = [c for c in range(width) if (c // dilation) % 2 == 0]
        inner = [c for c in firsts if c >= dilation and c + 2 * dilation < width]
        edge = [c for c in firsts if c not in inner]
        return inner, edge

    def forward_pair(number, column):
        dilation = 2**number
        summed = jnp.dot(
            gathered(levels[number], dilation, column),
            forward_w[number],
            preferred_element_type=F32,
        )
        for side in range(2):
            here = column + side * dilation
            z = summed[:, side * channels : (side + 1) * channels]
            sigma = 0.5 * jnp.tanh(0.5 * z) + 0.5
            act = z * sigma
            slope = sigma + act - act * sigma
            if number + 1 < LAYERS:
                slopes[number, here] = slope
                following = levels[number + 1]
                reach = 2 ** (number + 1)
                following[1, reach + here] = act.astype(BF16)
                fill(following, reach, reach + here, act)
            else:
                slabs[here] = act.astype(BF16)
                signal = columns_up[here].astype(F32) * slope
                signals[number][1, dilation + here] = signal.astype(BF16)
                fill(signals[number], dilation, dilation + here, signal)

    def backward_pair(number, column):
        dilation = 2**number
        back = lax.dot_general(
            gathered(signals[number], dilation, column),
            backward_w[number],
            (((1,), (1,)), ((), ())),
            preferred_element_type=F32,
        )
        for side in range(2):
            here = column + side * dilation
            value = back[:, side * channels : (side + 1) * channels]
            if number > 0:
                reach = dilation // 2
                value = value * slopes[number - 1, here]
                signals[number - 1][1, reach + here] = value.astype(BF16)
                fill(signals[number - 1], reach, reach + here, value)
            else:
                slabs[here] = value.astype(BF16)

    def run_layer(kind, number, pair, then_kind, then_number):
        dilation = 2**number
        inner, edge = pairs_of(dilation)
        for column in inner:
            pair(number, column)
        lefts = [c for c in edge if c < dilation]
        rights = [c for c in edge if c + 2 * dilation >= width]
        both = [c for c in lefts if c in rights]
        order = []
        if both:
            order = [both[i : i + 2] for i in range(0, len(both), 2)]
        else:
            order = [lefts[i : i + 2] for i in range(0, len(lefts), 2)]
            order += [rights[i : i + 2] for i in range(0, len(rights), 2)]
        for group in order:
            for column in group:
                if column < dilation:
                    receive(kind, number, 0, column)
                if column + 2 * dilation >= width:
                    receive(kind, number, 1, column + 2 * dilation - width)
            for column in group:
                pair(number, column)
            if then_number is not None:
                for column in group:
                    for here in (column, column + dilation):
                        send_column(then_kind, then_number, here)

    def weight_grad(number):
        dilation = 2**number
        signal = signals[number]
        lhs = jnp.concatenate(
            [
                signal[1, (2 - j) * dilation : (2 - j) * dilation + width].reshape(rows * width, channels)
                for j in range(3)
            ],
            axis=-1,
        )
        rhs = jnp.concatenate(
            [
                levels[number][i, dilation : dilation + width].reshape(rows * width, channels)
                for i in range(3)
            ],
            axis=-1,
        )
        total = lax.dot_general(lhs, rhs, (((0,), (0,)), ((), ())), preferred_element_type=F32)
        block = channels // ranks
        total = total.astype(BF16)
        for j in range(3):
            for i in range(3):
                piece = total[j * channels : (j + 1) * channels, i * channels : (i + 1) * channels]
                send_b[number, :, pl.ds((3 * i + j) * block, block), :] = piece.reshape(
                    ranks, block, channels
                )

    def batch_copy(number, step):
        target = lax.rem(batch + step, ranks)
        return pltpu.make_async_remote_copy(
            src_ref=send_b.at[number, target],
            dst_ref=recv_b.at[number, step],
            send_sem=batch_send.at[number, step],
            recv_sem=batch_recv.at[number, step],
            device_id={"batch": target},
            device_id_type=MESH,
        )

    def lon_copy(number, step):
        target = lax.rem(lon + step, groups)
        return pltpu.make_async_remote_copy(
            src_ref=send_l.at[number, target],
            dst_ref=recv_l.at[number, step],
            send_sem=lon_send.at[number, step],
            recv_sem=lon_recv.at[number, step],
            device_id={"lon": target},
            device_id_type=MESH,
        )

    def start_batch(number):
        @pl.loop(1, ranks)
        def _(step):
            batch_copy(number, step).start()

    def start_lon(number):
        @pl.loop(1, ranks)
        def _(step):
            batch_copy(number, step).wait_recv()

        total = send_b[number, batch].astype(F32)
        for step in range(1, ranks):
            total = total + recv_b[number, step].astype(F32)
        block = channels // ranks
        share = 9 * channels // groups
        lane = lax.broadcasted_iota(jnp.int32, (block, channels), 1)
        for target in range(groups):
            tap, offset = divmod(target * share, channels)
            value = total[tap * block : (tap + 1) * block]
            if offset:
                value = pltpu.roll(value, channels - offset, 1)
            if offset + share > channels:
                more = total[(tap + 1) * block : (tap + 2) * block]
                more = pltpu.roll(more, channels - offset, 1)
                value = jnp.where(lane < channels - offset, value, more)
            send_l[number, target] = value.astype(BF16)

        @pl.loop(1, groups)
        def _(step):
            lon_copy(number, step).start()

    def finish(number):
        @pl.loop(1, groups)
        def _(step):
            lon_copy(number, step).wait_recv()

        total = send_l[number, lon].astype(F32)
        for step in range(1, groups):
            total = total + recv_l[number, step].astype(F32)
        owned_ref[number] = total * (1.0 / math.sqrt(rows * width * groups * ranks))

    fetch_images.wait()
    level = levels[0]
    level[1, 1 : 1 + width] = swapped(staged[...])
    pl.semaphore_wait(barrier, groups + ranks - 2)
    send_column(0, 0, 0)
    send_column(0, 0, width - 1)
    edge_rows = jnp.zeros((PAD, channels), F32)
    for slot in range(shifter.shape[0]):
        shifter[slot, pl.ds(0, PAD), :] = edge_rows
        shifter[slot, pl.ds(PAD + rows, PAD), :] = edge_rows
    for column in range(width):
        fill(level, 1, 1 + column, level[1, 1 + column].astype(F32))
    fetch_taps.wait()
    build_forward(0)
    for number in range(LAYERS):
        if number + 1 < LAYERS:
            run_layer(0, number, forward_pair, 0, number + 1)
            build_forward(number + 1)
            if number == 0:
                fetch_upstream.wait()
                columns_up[...] = swapped(upstream[...])
        else:
            run_layer(0, number, forward_pair, 1, number)

    out_a[...] = swapped(slabs[...])
    store_features = pltpu.make_async_copy(out_a, features_ref, local_sem.at[3])
    store_features.start()
    for number in range(LAYERS):
        build_backward(number)
    for number in reversed(range(1, LAYERS)):
        run_layer(1, number, backward_pair, 1, number - 1)
        weight_grad(number)
        start_batch(number)
    start_lon(3)
    start_lon(2)
    receive(1, 0, 0, 0)
    receive(1, 0, 1, 0)
    weight_grad(0)
    start_batch(0)
    for column in range(0, width, 2):
        backward_pair(0, column)
    out_b[...] = swapped(slabs[...])
    store_grad = pltpu.make_async_copy(out_b, input_grad_ref, local_sem.at[4])
    store_grad.start()
    start_lon(1)
    start_lon(0)
    for number in reversed(range(LAYERS)):
        finish(number)

    for number in range(LAYERS):
        for kind in range(2):
            for side in range(2):
                for place in range(2**number):
                    halo_copy(kind, number, side, place).wait_send()

        @pl.loop(1, ranks)
        def _(step):
            batch_copy(number, step).wait_send()

        @pl.loop(1, groups)
        def _(step):
            lon_copy(number, step).wait_send()

    store_features.wait()
    store_grad.wait()


def local(images, weights, cotangent):
    _, rows, width, channels = images.shape
    groups, ranks = lax.axis_size("lon"), lax.axis_size("batch")
    block = channels // ranks
    field = (rows, width, channels)
    columns = (width, rows, channels)
    dilations = [2**number for number in range(LAYERS)]
    padded = [pltpu.VMEM((3, width + 2 * r, rows, channels), BF16) for r in dilations]
    features, input_grad, owned = pl.pallas_call(
        functools.partial(kernel, (groups, ranks)),
        out_shape=(
            jax.ShapeDtypeStruct(field, BF16),
            jax.ShapeDtypeStruct(field, BF16),
            jax.ShapeDtypeStruct((LAYERS, block, channels), F32),
        ),
        in_specs=[pl.BlockSpec(memory_space=pl.ANY)] * 3,
        out_specs=(
            pl.BlockSpec(memory_space=pl.ANY),
            pl.BlockSpec(memory_space=pl.ANY),
            pl.BlockSpec(memory_space=pltpu.VMEM),
        ),
        scratch_shapes=[
            pltpu.VMEM(field, BF16),
            pltpu.VMEM(field, BF16),
            pltpu.VMEM(columns, BF16),
            pltpu.VMEM((LAYERS, 9, channels, channels), BF16),
            pltpu.VMEM((LAYERS, 12 * channels, 2 * channels), BF16),
            pltpu.VMEM((LAYERS, 2 * channels, 12 * channels), BF16),
            pltpu.VMEM((width + 2 * dilations[-1], rows + 2 * PAD, channels), F32),
            pltpu.VMEM(columns, BF16),
            pltpu.VMEM(field, BF16),
            pltpu.VMEM(field, BF16),
            *padded,
            *padded,
            pltpu.VMEM((LAYERS - 1, *columns), F32),
            pltpu.VMEM((LAYERS, ranks, 9 * block, channels), BF16),
            pltpu.VMEM((LAYERS, ranks, 9 * block, channels), BF16),
            pltpu.VMEM((LAYERS, groups, block, channels), BF16),
            pltpu.VMEM((LAYERS, groups, block, channels), BF16),
            pltpu.SemaphoreType.DMA((5,)),
            pltpu.SemaphoreType.DMA((2, LAYERS, 2, dilations[-1])),
            pltpu.SemaphoreType.DMA((2, LAYERS, 2, dilations[-1])),
            pltpu.SemaphoreType.DMA((LAYERS, ranks)),
            pltpu.SemaphoreType.DMA((LAYERS, ranks)),
            pltpu.SemaphoreType.DMA((LAYERS, groups)),
            pltpu.SemaphoreType.DMA((LAYERS, groups)),
        ],
        compiler_params=pltpu.CompilerParams(
            collective_id=0, has_side_effects=True, vmem_limit_bytes=58 * 2**20
        ),
        name="panorama",
    )(images.reshape(field), weights, cotangent.reshape(field))
    share = 9 * channels // groups
    weight_grads = jnp.swapaxes(owned[:, :, :share], 1, 2)
    return features.reshape(images.shape), input_grad.reshape(images.shape), weight_grads


def solution(mesh):
    return jax.shard_map(
        local,
        mesh=mesh,
        in_specs=(P("batch", None, "lon", None), P(), P("batch", None, "lon", None)),
        out_specs=(
            P("batch", None, "lon", None),
            P("batch", None, "lon", None),
            P(None, "lon", "batch"),
        ),
        check_vma=False,
    )
```

time: 499 us -> 81 us (0.16); the launches traced: 491 us -> 80 us
  waiting for transfers between devices: 365 us -> 0 us
  Pallas kernels: 0 us -> 75.3 us
  starting transfers between devices: 48.6 us -> 0 us
  local copies, waits for them, and re-layouts: 27.8 us -> 4.1 us
  matrix products: 20.8 us -> 0 us
  between operations: 15.7 us -> 0.65 us
  other arithmetic: 12.4 us -> 0 us
    unnamed x6 -> x0, waiting for transfers between devices: 249 us -> none
    reduce_scatter x4 -> x0, waiting for transfers between devices: 114 us -> none  [local(): lax.psum_scatter(partial_term.astype(jnp.bfloat16), 'batch', scatter_dime...]
    pallas_call x0 -> x1, Pallas kernels: none -> 75.3 us  [local(): pl.pallas_call(functools.partial(kernel, (groups, ranks)), out_shape=(jax...]
    ppermute x16 -> x0, starting transfers between devices: 48.1 us -> none  [the longest x8 44.1 us: with_halo(): lax.ppermute(head, axis, [((i + 1) % count, i) for i in range(count)])]
    dot_general x12 -> x0, matrix products: 20.8 us -> none  [the longest x4 8.36 us: local(): jnp.einsum('bhwk,kc->bhwc', gather_taps(spread, dilation, columns), flipp...]
    unnamed x89 -> x4, local copies, waits for them, and re-layouts: 16.9 us -> 2.66 us
    slice x14 -> x0, local copies, waits for them, and re-layouts: 8.47 us -> none  [the longest x5 4.68 us: local(): flipped[number]]
    unnamed x22 -> x0, other arithmetic: 6.53 us -> none
  transfers between devices with their start and end apart: 21 -> 0, of which waited for: 9 -> 0; matrix products, arithmetic and copies ran while one was open for 7% -> 0% of each run, Pallas kernels for 0% -> 0%
where the time goes in v1:
time: 81 us; the launch traced here: 80 us
  Pallas kernels  75.3 us (93%)
  local copies, waits for them, and re-layouts  4.1 us (5%)
    pallas_call x1, Pallas kernels, local(): pl.pallas_call(functools.partial(kernel, (groups, ranks)), out_shape=(jax...  75.3 us
    unnamed x4, local copies, waits for them, and re-layouts  2.66 us

profile of v1, /device:TPU:1, one launch (start us, length us, event | category | flops | bytes accessed | tf_op | source)
XLA Modules:
  0.0 80.0 jit_solution(2848420024374109759)
XLA Ops:
  0.6 75.3 %panorama.1 = (bf16[128,16,128]{2,1,0:T(8,128)(2,1)}, bf16[128,16,128]{2,1,0:T(8,128)(2,1)}, f32[4,16,128]{2,1,0:T(8,128)}) custom-call(bf16[128,16,128]{2,1,0:T(8,128)(2,1)} %bitcast.6, bf16[4,9,128,128]{3,2,1,0:T(8,128)(2,1)} %weights_ref.1, bf16[128,16,128]{2,1,0:T(8,128)(2,1)} %bitcast.7), custom_call_target="tpu_custom_call" | custom-call | tf_op jit(solution)/shard_map/panorama/pallas_call | solution.py:371
  75.9 0.0 copy-start
  75.9 1.4 %slice_bitcast_fusion = f32[4,36,16]{1,2,0:T(8,128)} fusion(f32[4,16,128]{2,1,0:T(8,128)} %get-tuple-element.8), kind=kLoop, calls=%fused_computation | loop fusion | bytes 18432 | tf_op jit(solution)/shard_map/transpose | solution.py:416
  77.3 1.9 %copy.8 = bf16[1,128,16,128]{3,2,1,0:T(8,128)(2,1)} copy(bf16[1,128,16,128]{3,2,1,0:T(8,128)(2,1)} %bitcast.9) | data formatting | bytes 1048576
  79.2 0.0 copy-done
  79.2 0.8 copy.9
Async XLA Ops:
  75.9 3.3 %copy-start = (bf16[128,16,128]{2,1,0:T(8,128)(2,1)S(1)}, bf16[128,16,128]{2,1,0:T(8,128)(2,1)}, u32[]{:S(2)}) copy-start(bf16[128,16,128]{2,1,0:T(8,128)(2,1)} %get-tuple-element.7) | copy-start | bytes 1572868

commit v2 on v1

v2 whole, which is shorter than its diff:
```python
import functools
import math

import jax
import jax.numpy as jnp
from jax import lax
from jax.experimental import pallas as pl
from jax.experimental.pallas import tpu as pltpu
from jax.sharding import PartitionSpec as P

LAYERS = 4
PAD = 8
BF16 = jnp.bfloat16
F32 = jnp.float32
MESH = pl.DeviceIdType.MESH

LEVEL_PAD = (7, 6, 4, 8)
SIGNAL_PAD = (1, 2, 6, 8)
SLOPE_PAD = (0, 2, 0)
PIECES = (
    (((0, 1), (1, 2), (3, 2), (5, 2)), ((15, 1), (13, 2), (11, 2), (9, 2))),
    (((0, 2), (4, 2), (2, 2), (6, 2)), ((8, 2), (12, 2), (10, 2), (14, 2))),
    (((0, 2), (4, 2), (2, 2), (6, 2)), ((8, 2), (12, 2), (10, 2), (14, 2))),
    (((0, 2), (4, 2), (2, 2)), ((12, 2), (10, 2), (14, 2))),
    (((0, 1),), ((15, 1),)),
)


def swapped(value):
    return jnp.swapaxes(value, 0, 1)


def kernel(
    ring, images_ref, weights_ref, cotangent_ref, features_ref, input_grad_ref, owned_ref, *scratch
):
    groups, ranks = ring
    (staged, upstream, columns_up, taps, forward_w, backward_w, shifter, slabs) = scratch[:8]
    levels = scratch[8:12]
    signals = scratch[12:16]
    slopes = scratch[16:19]
    send_b, recv_b, send_l, recv_l, send_m, recv_m, local_sem = scratch[19:26]
    halo_send, halo_recv, batch_send, batch_recv, lon_send, lon_recv = scratch[26:32]

    lon = lax.axis_index("lon")
    batch = lax.axis_index("batch")
    right, left = lax.rem(lon + 1, groups), lax.rem(lon + groups - 1, groups)
    rows, width, channels = staged.shape
    block = channels // ranks
    share = 9 * channels // groups

    fetch_images = pltpu.make_async_copy(images_ref, staged, local_sem.at[0])
    fetch_taps = pltpu.make_async_copy(weights_ref, taps, local_sem.at[1])
    fetch_upstream = pltpu.make_async_copy(cotangent_ref, upstream, local_sem.at[2])
    fetch_images.start()
    fetch_taps.start()
    fetch_upstream.start()

    barrier = pltpu.get_barrier_semaphore()

    @pl.loop(1, groups)
    def _(step):
        pl.semaphore_signal(
            barrier, inc=1, device_id={"lon": lax.rem(lon + step, groups)}, device_id_type=MESH
        )

    @pl.loop(1, ranks)
    def _(step):
        pl.semaphore_signal(
            barrier, inc=1, device_id={"batch": lax.rem(batch + step, ranks)}, device_id_type=MESH
        )

    exchanged = (
        (levels[0], LEVEL_PAD[0]),
        (levels[3], LEVEL_PAD[3]),
        (signals[3], SIGNAL_PAD[3]),
        (signals[2], SIGNAL_PAD[2]),
        (signals[0], SIGNAL_PAD[0]),
    )

    def halo_copy(which, side, piece):
        buffer, pad = exchanged[which]
        first, count = PIECES[which][side][piece]
        landing = first + width if side == 0 else first - width
        return pltpu.make_async_remote_copy(
            src_ref=buffer.at[1, pad + first : pad + first + count],
            dst_ref=buffer.at[1, pad + landing : pad + landing + count],
            send_sem=halo_send.at[which, side, piece],
            recv_sem=halo_recv.at[which, side, piece],
            device_id={"lon": left if side == 0 else right},
            device_id_type=MESH,
        )

    def fill(buffer, dilation, slot, value):
        shifter[slot, pl.ds(PAD, rows), :] = value
        buffer[0, slot] = shifter[slot, pl.ds(PAD - dilation, rows), :].astype(BF16)
        buffer[2, slot] = shifter[slot, pl.ds(PAD + dilation, rows), :].astype(BF16)

    def receive(which, side, piece, dilation):
        buffer, pad = exchanged[which]
        halo_copy(which, side, piece).wait_recv()
        first, count = PIECES[which][side][piece]
        landing = pad + (first + width if side == 0 else first - width)
        for slot in range(landing, landing + count):
            fill(buffer, dilation, slot, buffer[1, slot].astype(F32))

    def tap_block(number, tap_row, tap_column, turned):
        if not 0 <= tap_column < 3:
            return jnp.zeros((channels, channels), BF16)
        tap = 3 * tap_row + tap_column
        return taps[number, 8 - tap if turned else tap]

    def build_forward(number):
        for span in range(4):
            for row in range(3):
                for side in range(2):
                    forward_w[
                        number,
                        pl.ds((3 * span + row) * channels, channels),
                        pl.ds(side * channels, channels),
                    ] = tap_block(number, row, span - side, False)

    def build_backward(number):
        for span in range(4):
            for row in range(3):
                for side in range(2):
                    backward_w[
                        number,
                        pl.ds(side * channels, channels),
                        pl.ds((3 * span + row) * channels, channels),
                    ] = tap_block(number, row, span - side, True)

    def gathered(buffer, pad, dilation, column, spans=4):
        return jnp.concatenate(
            [
                buffer[row, pad + column + (span - 1) * dilation]
                for span in range(spans)
                for row in range(3)
            ],
            axis=-1,
        )

    def forward_pair(number, column):
        dilation = 2**number
        summed = jnp.dot(
            gathered(levels[number], LEVEL_PAD[number], dilation, column),
            forward_w[number],
            preferred_element_type=F32,
        )
        for side in range(2):
            here = column + side * dilation
            z = summed[:, side * channels : (side + 1) * channels]
            sigma = 0.5 * jnp.tanh(0.5 * z) + 0.5
            act = z * sigma
            if number + 1 < LAYERS:
                if -SLOPE_PAD[number] <= here < width + SLOPE_PAD[number]:
                    slopes[number][SLOPE_PAD[number] + here] = sigma + act - act * sigma
                following, slot = levels[number + 1], LEVEL_PAD[number + 1] + here
                following[1, slot] = act.astype(BF16)
                fill(following, 2 * dilation, slot, act)
            else:
                slabs[here] = act.astype(BF16)
                signal = columns_up[here].astype(F32) * (sigma + act - act * sigma)
                slot = SIGNAL_PAD[number] + here
                signals[number][1, slot] = signal.astype(BF16)
                fill(signals[number], dilation, slot, signal)

    def backward_columns(number, column, sides):
        dilation = 2**number
        spans = 2 + sides
        back = lax.dot_general(
            gathered(signals[number], SIGNAL_PAD[number], dilation, column, spans),
            backward_w[number, pl.ds(0, sides * channels), pl.ds(0, 3 * spans * channels)],
            (((1,), (1,)), ((), ())),
            preferred_element_type=F32,
        )
        for side in range(sides):
            here = column + side * dilation
            value = back[:, side * channels : (side + 1) * channels]
            if number > 0:
                value = value * slopes[number - 1][SLOPE_PAD[number - 1] + here]
                slot = SIGNAL_PAD[number - 1] + here
                signals[number - 1][1, slot] = value.astype(BF16)
                fill(signals[number - 1], dilation // 2, slot, value)
            else:
                slabs[here] = value.astype(BF16)

    def weight_grad(number):
        dilation = 2**number
        signal, pad, level_pad = signals[number], SIGNAL_PAD[number], LEVEL_PAD[number]
        lhs = jnp.concatenate(
            [
                signal[1, pad + (1 - j) * dilation : pad + (1 - j) * dilation + width].reshape(
                    rows * width, channels
                )
                for j in range(3)
            ],
            axis=-1,
        )
        rhs = jnp.concatenate(
            [
                levels[number][i, level_pad : level_pad + width].reshape(rows * width, channels)
                for i in range(3)
            ],
            axis=-1,
        )
        total = lax.dot_general(lhs, rhs, (((0,), (0,)), ((), ())), preferred_element_type=F32)
        total = total.astype(BF16)
        for j in range(3):
            for i in range(3):
                piece = total[j * channels : (j + 1) * channels, i * channels : (i + 1) * channels]
                send_b[number, :, pl.ds((3 * i + j) * block, block), :] = piece.reshape(
                    ranks, block, channels
                )

    def batch_copy(number, step):
        target = lax.rem(batch + step, ranks)
        return pltpu.make_async_remote_copy(
            src_ref=send_b.at[number, target],
            dst_ref=recv_b.at[number, step],
            send_sem=batch_send.at[number, step],
            recv_sem=batch_recv.at[number, step],
            device_id={"batch": target},
            device_id_type=MESH,
        )

    sets = ((send_l, recv_l, (0,)), (send_m, recv_m, (3, 2, 1)))

    def lon_copy(which, step):
        source, landing, _ = sets[which]
        target = lax.rem(lon + step, groups)
        return pltpu.make_async_remote_copy(
            src_ref=source.at[target],
            dst_ref=landing.at[step],
            send_sem=lon_send.at[which, step],
            recv_sem=lon_recv.at[which, step],
            device_id={"lon": target},
            device_id_type=MESH,
        )

    def start_batch(number):
        @pl.loop(1, ranks)
        def _(step):
            batch_copy(number, step).start()

    lane = lax.broadcasted_iota(jnp.int32, (block, channels), 1)

    def prepare_lon(which):
        source, _, numbers = sets[which]
        for place, number in enumerate(numbers):

            @pl.loop(1, ranks)
            def _(step):
                batch_copy(number, step).wait_recv()

            total = send_b[number, batch].astype(F32)
            for step in range(1, ranks):
                total = total + recv_b[number, step].astype(F32)
            for target in range(groups):
                tap, offset = divmod(target * share, channels)
                value = total[tap * block : (tap + 1) * block]
                if offset:
                    value = pltpu.roll(value, channels - offset, 1)
                if offset + share > channels:
                    more = total[(tap + 1) * block : (tap + 2) * block]
                    more = pltpu.roll(more, channels - offset, 1)
                    value = jnp.where(lane < channels - offset, value, more)
                source[target, pl.ds(place * block, block), :] = value.astype(BF16)

    def start_lon(which):
        prepare_lon(which)

        @pl.loop(1, groups)
        def _(step):
            lon_copy(which, step).start()

    def finish(which):
        @pl.loop(1, groups)
        def _(step):
            lon_copy(which, step).wait_recv()

        source, landing, numbers = sets[which]
        total = source[lon].astype(F32)
        for step in range(1, groups):
            total = total + landing[step].astype(F32)
        total = total * (1.0 / math.sqrt(rows * width * groups * ranks))
        for place, number in enumerate(numbers):
            owned_ref[number] = total[place * block : (place + 1) * block, :share]

    fetch_images.wait()
    level, pad = levels[0], LEVEL_PAD[0]
    level[1, pad : pad + width] = swapped(staged[...])
    pl.semaphore_wait(barrier, groups + ranks - 2)
    for piece in range(4):
        for side in range(2):
            halo_copy(0, side, piece).start()
    edge_rows = jnp.zeros((PAD, channels), F32)
    for slot in range(shifter.shape[0]):
        shifter[slot, pl.ds(0, PAD), :] = edge_rows
        shifter[slot, pl.ds(PAD + rows, PAD), :] = edge_rows
    for column in range(width):
        fill(level, 1, pad + column, level[1, pad + column].astype(F32))
    fetch_taps.wait()
    build_forward(0)
    for column in range(2, width - 2, 2):
        forward_pair(0, column)
    build_forward(1)
    for column in (4, 5, 8, 9):
        forward_pair(1, column)
    fetch_upstream.wait()
    columns_up[...] = swapped(upstream[...])
    for number in (2, 3):
        build_forward(number)
    for piece in range(4):
        receive(0, 0, piece, 1)
        receive(0, 1, piece, 1)
        forward_pair(0, -2 * piece)
        forward_pair(0, width - 2 + 2 * piece)
        if piece == 1:
            for column in (0, 1, 12, 13):
                forward_pair(1, column)
    for column in (-4, -3, 16, 17):
        forward_pair(1, column)
    for first in (0, 2):
        for side in range(2):
            for column in (first, first + 1):
                forward_pair(2, column + 8 * side)
            halo_copy(1, side, first).start()
            halo_copy(1, side, first + 1).start()
    for number in range(LAYERS):
        build_backward(number)
    for piece, first in enumerate((0, 4, 2, 6)):
        receive(1, 0, piece, 8)
        receive(1, 1, piece, 8)
        forward_pair(3, first)
        forward_pair(3, first + 1)
        halo_copy(2, 0, piece).start()
        halo_copy(2, 1, piece).start()

    features_ref[...] = swapped(slabs[...])
    ready = (((0, 0),), ((0, 1), (1, 0)), ((0, 2), (1, 1)), ((1, 2),))
    for piece, first in enumerate((0, 4, 2, 6)):
        receive(2, 0, piece, 8)
        receive(2, 1, piece, 8)
        backward_columns(3, first, 2)
        backward_columns(3, first + 1, 2)
        for side, part in ready[piece]:
            halo_copy(3, side, part).start()
    weight_grad(3)
    start_batch(3)
    for side in range(2):
        for piece in range(3):
            receive(3, side, piece, 4)
    for column in (0, 1, 2, 3, 8, 9, 10, 11):
        backward_columns(2, column, 2)
    for column in (-2, -1, 16, 17):
        backward_columns(2, column, 1)
    for column in (0, 13):
        backward_columns(1, column, 2)
    halo_copy(4, 0, 0).start()
    halo_copy(4, 1, 0).start()
    for column in (1, 4, 5, 8, 9, 12):
        backward_columns(1, column, 2)
    weight_grad(2)
    start_batch(2)
    weight_grad(1)
    start_batch(1)
    receive(4, 0, 0, 1)
    receive(4, 1, 0, 1)
    weight_grad(0)
    start_batch(0)
    for column in range(0, width, 2):
        backward_columns(0, column, 2)
    input_grad_ref[...] = swapped(slabs[...])
    start_lon(1)
    start_lon(0)
    finish(1)
    finish(0)

    for which in range(len(PIECES)):
        for side in range(2):
            for piece in range(len(PIECES[which][side])):
                halo_copy(which, side, piece).wait_send()
    for number in range(LAYERS):

        @pl.loop(1, ranks)
        def _(step):
            batch_copy(number, step).wait_send()

    for which in range(2):

        @pl.loop(1, groups)
        def _(step):
            lon_copy(which, step).wait_send()


def local(images, weights, cotangent):
    _, rows, width, channels = images.shape
    groups, ranks = lax.axis_size("lon"), lax.axis_size("batch")
    block = channels // ranks
    share = 9 * channels // groups
    field = (rows, width, channels)

    def columns(pad, *front):
        return (*front, width + 2 * pad, rows, channels)

    features, input_grad, owned = pl.pallas_call(
        functools.partial(kernel, (groups, ranks)),
        out_shape=(
            pltpu.VMEM(field, BF16),
            pltpu.VMEM(field, BF16),
            pltpu.VMEM((LAYERS, block, share), F32),
        ),
        in_specs=[pl.BlockSpec(memory_space=pl.ANY)] * 3,
        out_specs=(pl.BlockSpec(memory_space=pltpu.VMEM),) * 3,
        scratch_shapes=[
            pltpu.VMEM(field, BF16),
            pltpu.VMEM(field, BF16),
            pltpu.VMEM(columns(0), BF16),
            pltpu.VMEM((LAYERS, 9, channels, channels), BF16),
            pltpu.VMEM((LAYERS, 12 * channels, 2 * channels), BF16),
            pltpu.VMEM((LAYERS, 2 * channels, 12 * channels), BF16),
            pltpu.VMEM((width + 2 * max(LEVEL_PAD), rows + 2 * PAD, channels), F32),
            pltpu.VMEM(columns(0), BF16),
            *[pltpu.VMEM(columns(pad, 3), BF16) for pad in LEVEL_PAD],
            *[pltpu.VMEM(columns(pad, 3), BF16) for pad in SIGNAL_PAD],
            *[pltpu.VMEM(columns(pad), F32) for pad in SLOPE_PAD],
            pltpu.VMEM((LAYERS, ranks, 9 * block, channels), BF16),
            pltpu.VMEM((LAYERS, ranks, 9 * block, channels), BF16),
            pltpu.VMEM((groups, block, channels), BF16),
            pltpu.VMEM((groups, block, channels), BF16),
            pltpu.VMEM((groups, 3 * block, channels), BF16),
            pltpu.VMEM((groups, 3 * block, channels), BF16),
            pltpu.SemaphoreType.DMA((3,)),
            pltpu.SemaphoreType.DMA((len(PIECES), 2, 4)),
            pltpu.SemaphoreType.DMA((len(PIECES), 2, 4)),
            pltpu.SemaphoreType.DMA((LAYERS, ranks)),
            pltpu.SemaphoreType.DMA((LAYERS, ranks)),
            pltpu.SemaphoreType.DMA((2, groups)),
            pltpu.SemaphoreType.DMA((2, groups)),
        ],
        compiler_params=pltpu.CompilerParams(
            collective_id=0, has_side_effects=True, vmem_limit_bytes=58 * 2**20
        ),
        name="panorama",
    )(images.reshape(field), weights, cotangent.reshape(field))
    weight_grads = jnp.swapaxes(owned, 1, 2)
    return features.reshape(images.shape), input_grad.reshape(images.shape), weight_grads


def solution(mesh):
    return jax.shard_map(
        local,
        mesh=mesh,
        in_specs=(P("batch", None, "lon", None), P(), P("batch", None, "lon", None)),
        out_specs=(
            P("batch", None, "lon", None),
            P("batch", None, "lon", None),
            P(None, "lon", "batch"),
        ),
        check_vma=False,
    )
```

time: 81 us -> 68 us (0.84)
  Pallas kernels: 75.3 us -> 64 us
  local copies, waits for them, and re-layouts: 4.1 us -> 2.2 us
    pallas_call x1, Pallas kernels: 75.3 us -> 64 us  [local(): pl.pallas_call(functools.partial(kernel, (groups, ranks)), out_shape=(plt...]
    transpose x1 -> x0, local copies, waits for them, and re-layouts: 1.43 us -> none  [local(): weight_grads = jnp.swapaxes(owned[:, :, :share], 1, 2)]
    unnamed x4 -> x3, local copies, waits for them, and re-layouts: 2.66 us -> 2.2 us
where the time goes in v2:
time: 68 us; the launch traced here: 66.9 us
  Pallas kernels  64 us (94%)
  local copies, waits for them, and re-layouts  2.2 us (3%)
    pallas_call x1, Pallas kernels, local(): pl.pallas_call(functools.partial(kernel, (groups, ranks)), out_shape=(plt...  64 us
    unnamed x3, local copies, waits for them, and re-layouts  2.2 us

profile of v2, /device:TPU:1, one launch (start us, length us, event | category | flops | bytes accessed | tf_op | source)
XLA Modules:
  0.0 66.9 jit_solution(15820742794743850312)
XLA Ops:
  0.6 64.0 %panorama.1 = (bf16[128,16,128]{2,1,0:T(8,128)(2,1)S(1)}, bf16[128,16,128]{2,1,0:T(8,128)(2,1)S(1)}, f32[4,16,36]{2,1,0:T(8,128)S(1)}) custom-call(bf16[128,16,128]{2,1,0:T(8,128)(2,1)} %bitcast.8, bf16[4,9,128,128]{3,2,1,0:T(8,128)(2,1)} %weights_ref.1, bf16[128,16,128]{2,1,0:T(8,128)(2,1)} %bitcast.9), custom_call_target="tpu_custom_call" | custom-call | tf_op jit(solution)/shard_map/panorama/pallas_call | solution.py:406
  64.7 0.8 %copy.9 = bf16[1,128,16,128]{3,2,1,0:T(8,128)(2,1)} copy(bf16[1,128,16,128]{3,2,1,0:T(8,128)(2,1)S(1)} %bitcast.6) | data formatting | bytes 1048576
  65.5 0.8 %copy.10 = bf16[1,128,16,128]{3,2,1,0:T(8,128)(2,1)} copy(bf16[1,128,16,128]{3,2,1,0:T(8,128)(2,1)S(1)} %bitcast.5) | data formatting | bytes 1048576
  66.3 0.6 copy.11

commit v3 on v2

--- a/solution.py
+++ b/solution.py
@@ -38,8 +38,8 @@
     levels = scratch[8:12]
     signals = scratch[12:16]
     slopes = scratch[16:19]
-    send_b, recv_b, send_l, recv_l, send_m, recv_m, local_sem = scratch[19:26]
-    halo_send, halo_recv, batch_send, batch_recv, lon_send, lon_recv = scratch[26:32]
+    send_b, recv_b, send_l, recv_l, local_sem = scratch[19:24]
+    halo_send, halo_recv, batch_send, batch_recv, lon_send, lon_recv = scratch[24:30]
 
     lon = lax.axis_index("lon")
     batch = lax.axis_index("batch")
@@ -186,105 +186,92 @@
 
     def weight_grad(number):
         dilation = 2**number
-        signal, pad, level_pad = signals[number], SIGNAL_PAD[number], LEVEL_PAD[number]
-        lhs = jnp.concatenate(
-            [
-                signal[1, pad + (1 - j) * dilation : pad + (1 - j) * dilation + width].reshape(
-                    rows * width, channels
-                )
-                for j in range(3)
-            ],
-            axis=-1,
-        )
-        rhs = jnp.concatenate(
-            [
-                levels[number][i, level_pad : level_pad + width].reshape(rows * width, channels)
-                for i in range(3)
-            ],
-            axis=-1,
-        )
-        total = lax.dot_general(lhs, rhs, (((0,), (0,)), ((), ())), preferred_element_type=F32)
-        total = total.astype(BF16)
+        pad, level_pad = SIGNAL_PAD[number], LEVEL_PAD[number]
+        signal = signals[number][1, pad : pad + width].reshape(rows * width, channels)
         for j in range(3):
+            first = level_pad + (j - 1) * dilation
+            taken = jnp.concatenate(
+                [
+                    levels[number][i, first : first + width].reshape(rows * width, channels)
+                    for i in range(3)
+                ],
+                axis=-1,
+            )
+            total = lax.dot_general(
+                signal, taken, (((0,), (0,)), ((), ())), preferred_element_type=F32
+            ).astype(BF16)
             for i in range(3):
-                piece = total[j * channels : (j + 1) * channels, i * channels : (i + 1) * channels]
-                send_b[number, :, pl.ds((3 * i + j) * block, block), :] = piece.reshape(
-                    ranks, block, channels
-                )
-
-    def batch_copy(number, step):
-        target = lax.rem(batch + step, ranks)
-        return pltpu.make_async_remote_copy(
-            src_ref=send_b.at[number, target],
-            dst_ref=recv_b.at[number, step],
-            send_sem=batch_send.at[number, step],
-            recv_sem=batch_recv.at[number, step],
-            device_id={"batch": target},
-            device_id_type=MESH,
-        )
-
-    sets = ((send_l, recv_l, (0,)), (send_m, recv_m, (3, 2, 1)))
-
-    def lon_copy(which, step):
-        source, landing, _ = sets[which]
-        target = lax.rem(lon + step, groups)
-        return pltpu.make_async_remote_copy(
-            src_ref=source.at[target],
-            dst_ref=landing.at[step],
-            send_sem=lon_send.at[which, step],
-            recv_sem=lon_recv.at[which, step],
-            device_id={"lon": target},
-            device_id_type=MESH,
-        )
+                send_b[number, :, pl.ds((3 * i + j) * block, block), :] = total[
+                    :, i * channels : (i + 1) * channels
+                ].reshape(ranks, block, channels)
 
     def start_batch(number):
-        @pl.loop(1, ranks)
-        def _(step):
-            batch_copy(number, step).start()
+        half = ranks // 4
+        for step in (half, 3 * half, *(n for n in range(1, ranks) if n not in (half, 3 * half))):
+            target = lax.rem(batch + step, ranks)
+            pltpu.make_async_remote_copy(
+                src_ref=send_b.at[number, target],
+                dst_ref=recv_b.at[number, step],
+                send_sem=batch_send.at[number],
+                recv_sem=batch_recv.at[number],
+                device_id={"batch": target},
+                device_id_type=MESH,
+            ).start()
+
+    sets = ((3, 2), (0, 1))
 
     lane = lax.broadcasted_iota(jnp.int32, (block, channels), 1)
 
-    def prepare_lon(which):
-        source, _, numbers = sets[which]
-        for place, number in enumerate(numbers):
-
-            @pl.loop(1, ranks)
-            def _(step):
-                batch_copy(number, step).wait_recv()
-
+    def start_lon(which):
+        totals = []
+        for number in sets[which]:
+            arrived = recv_b.at[number, 1:]
+            pltpu.make_async_copy(arrived, arrived, batch_recv.at[number]).wait()
             total = send_b[number, batch].astype(F32)
             for step in range(1, ranks):
                 total = total + recv_b[number, step].astype(F32)
-            for target in range(groups):
-                tap, offset = divmod(target * share, channels)
-                value = total[tap * block : (tap + 1) * block]
-                if offset:
-                    value = pltpu.roll(value, channels - offset, 1)
+            totals.append(total)
+
+        def shifted(total, tap, amount):
+            value = total[tap * block : (tap + 1) * block]
+            return pltpu.roll(value, amount, 1) if amount else value
+
+        for target in range(groups):
+            tap, offset = divmod(target * share, channels)
+            packed = None
+            for place, total in enumerate(totals):
+                amount = (place * share - offset) % channels
+                value = shifted(total, tap, amount)
                 if offset + share > channels:
-                    more = total[(tap + 1) * block : (tap + 2) * block]
-                    more = pltpu.roll(more, channels - offset, 1)
-                    value = jnp.where(lane < channels - offset, value, more)
-                source[target, pl.ds(place * block, block), :] = value.astype(BF16)
-
-    def start_lon(which):
-        prepare_lon(which)
-
-        @pl.loop(1, groups)
-        def _(step):
-            lon_copy(which, step).start()
+                    more = shifted(total, tap + 1, amount)
+                    value = jnp.where(lane < place * share + channels - offset, value, more)
+                packed = value if packed is None else jnp.where(lane < place * share, packed, value)
+            send_l[which, target] = packed.astype(BF16)
+
+        @pl.loop(0, groups - 1)
+        def _(turn):
+            rank = turn // 2
+            apart = ((rank + 1) // 2) * (2 * (rank % 2) - 1)
+            step = (groups // 4 + (turn % 2) * (groups // 2) + apart + groups) % groups
+            target = lax.rem(lon + step, groups)
+            pltpu.make_async_remote_copy(
+                src_ref=send_l.at[which, target],
+                dst_ref=recv_l.at[which, step],
+                send_sem=lon_send.at[which],
+                recv_sem=lon_recv.at[which],
+                device_id={"lon": target},
+                device_id_type=MESH,
+            ).start()
 
     def finish(which):
-        @pl.loop(1, groups)
-        def _(step):
-            lon_copy(which, step).wait_recv()
-
-        source, landing, numbers = sets[which]
-        total = source[lon].astype(F32)
+        arrived = recv_l.at[which, 1:]
+        pltpu.make_async_copy(arrived, arrived, lon_recv.at[which]).wait()
+        total = send_l[which, lon].astype(F32)
         for step in range(1, groups):
-            total = total + landing[step].astype(F32)
+            total = total + recv_l[which, step].astype(F32)
         total = total * (1.0 / math.sqrt(rows * width * groups * ranks))
-        for place, number in enumerate(numbers):
-            owned_ref[number] = total[place * block : (place + 1) * block, :share]
+        for place, number in enumerate(sets[which]):
+            owned_ref[number] = total[:, place * share : (place + 1) * share]
 
     fetch_images.wait()
     level, pad = levels[0], LEVEL_PAD[0]
@@ -310,16 +297,15 @@
     columns_up[...] = swapped(upstream[...])
     for number in (2, 3):
         build_forward(number)
-    for piece in range(4):
-        receive(0, 0, piece, 1)
-        receive(0, 1, piece, 1)
-        forward_pair(0, -2 * piece)
-        forward_pair(0, width - 2 + 2 * piece)
-        if piece == 1:
-            for column in (0, 1, 12, 13):
-                forward_pair(1, column)
-    for column in (-4, -3, 16, 17):
-        forward_pair(1, column)
+    for half in range(2):
+        for piece in (2 * half, 2 * half + 1):
+            receive(0, 0, piece, 1)
+            receive(0, 1, piece, 1)
+        for piece in (2 * half, 2 * half + 1):
+            forward_pair(0, -2 * piece)
+            forward_pair(0, width - 2 + 2 * piece)
+        for column in ((0, 1, 12, 13), (-4, -3, 16, 17))[half]:
+            forward_pair(1, column)
     for first in (0, 2):
         for side in range(2):
             for column in (first, first + 1):
@@ -328,25 +314,31 @@
             halo_copy(1, side, first + 1).start()
     for number in range(LAYERS):
         build_backward(number)
-    for piece, first in enumerate((0, 4, 2, 6)):
-        receive(1, 0, piece, 8)
-        receive(1, 1, piece, 8)
-        forward_pair(3, first)
-        forward_pair(3, first + 1)
-        halo_copy(2, 0, piece).start()
-        halo_copy(2, 1, piece).start()
+    for half, columns in enumerate(((0, 1, 4, 5), (2, 3, 6, 7))):
+        for piece in (2 * half, 2 * half + 1):
+            receive(1, 0, piece, 8)
+            receive(1, 1, piece, 8)
+        for place, column in enumerate(columns):
+            forward_pair(3, column)
+            if place % 2:
+                halo_copy(2, 0, 2 * half + place // 2).start()
+                halo_copy(2, 1, 2 * half + place // 2).start()
 
     features_ref[...] = swapped(slabs[...])
     ready = (((0, 0),), ((0, 1), (1, 0)), ((0, 2), (1, 1)), ((1, 2),))
-    for piece, first in enumerate((0, 4, 2, 6)):
-        receive(2, 0, piece, 8)
-        receive(2, 1, piece, 8)
-        backward_columns(3, first, 2)
-        backward_columns(3, first + 1, 2)
-        for side, part in ready[piece]:
-            halo_copy(3, side, part).start()
+    for half, columns in enumerate(((0, 1, 4, 5), (2, 3, 6, 7))):
+        for piece in (2 * half, 2 * half + 1):
+            receive(2, 0, piece, 8)
+            receive(2, 1, piece, 8)
+        for place, column in enumerate(columns):
+            backward_columns(3, column, 2)
+            if place % 2:
+                for side, part in ready[2 * half + place // 2]:
+                    halo_copy(3, side, part).start()
     weight_grad(3)
     start_batch(3)
+    weight_grad(2)
+    start_batch(2)
     for side in range(2):
         for piece in range(3):
             receive(3, side, piece, 4)
@@ -354,43 +346,35 @@
         backward_columns(2, column, 2)
     for column in (-2, -1, 16, 17):
         backward_columns(2, column, 1)
-    for column in (0, 13):
+    for column in (0, 13, 1, 4, 5, 8, 9, 12):
         backward_columns(1, column, 2)
-    halo_copy(4, 0, 0).start()
-    halo_copy(4, 1, 0).start()
-    for column in (1, 4, 5, 8, 9, 12):
-        backward_columns(1, column, 2)
-    weight_grad(2)
-    start_batch(2)
+        if column == 13:
+            halo_copy(4, 0, 0).start()
+            halo_copy(4, 1, 0).start()
+    weight_grad(0)
+    start_batch(0)
     weight_grad(1)
     start_batch(1)
+    start_lon(0)
     receive(4, 0, 0, 1)
     receive(4, 1, 0, 1)
-    weight_grad(0)
-    start_batch(0)
     for column in range(0, width, 2):
         backward_columns(0, column, 2)
     input_grad_ref[...] = swapped(slabs[...])
     start_lon(1)
-    start_lon(0)
+    finish(0)
     finish(1)
-    finish(0)
 
     for which in range(len(PIECES)):
         for side in range(2):
             for piece in range(len(PIECES[which][side])):
                 halo_copy(which, side, piece).wait_send()
     for number in range(LAYERS):
-
-        @pl.loop(1, ranks)
-        def _(step):
-            batch_copy(number, step).wait_send()
-
+        sent = send_b.at[number, 1:]
+        pltpu.make_async_copy(sent, sent, batch_send.at[number]).wait()
     for which in range(2):
-
-        @pl.loop(1, groups)
-        def _(step):
-            lon_copy(which, step).wait_send()
+        sent = send_l.at[which, 1:]
+        pltpu.make_async_copy(sent, sent, lon_send.at[which]).wait()
 
 
 def local(images, weights, cotangent):
@@ -426,17 +410,15 @@
             *[pltpu.VMEM(columns(pad), F32) for pad in SLOPE_PAD],
             pltpu.VMEM((LAYERS, ranks, 9 * block, channels), BF16),
             pltpu.VMEM((LAYERS, ranks, 9 * block, channels), BF16),
-            pltpu.VMEM((groups, block, channels), BF16),
-            pltpu.VMEM((groups, block, channels), BF16),
-            pltpu.VMEM((groups, 3 * block, channels), BF16),
-            pltpu.VMEM((groups, 3 * block, channels), BF16),
+            pltpu.VMEM((2, groups, block, channels), BF16),
+            pltpu.VMEM((2, groups, block, channels), BF16),
             pltpu.SemaphoreType.DMA((3,)),
             pltpu.SemaphoreType.DMA((len(PIECES), 2, 4)),
             pltpu.SemaphoreType.DMA((len(PIECES), 2, 4)),
-            pltpu.SemaphoreType.DMA((LAYERS, ranks)),
-            pltpu.SemaphoreType.DMA((LAYERS, ranks)),
-            pltpu.SemaphoreType.DMA((2, groups)),
-            pltpu.SemaphoreType.DMA((2, groups)),
+            pltpu.SemaphoreType.DMA((LAYERS,)),
+            pltpu.SemaphoreType.DMA((LAYERS,)),
+            pltpu.SemaphoreType.DMA((2,)),
+            pltpu.SemaphoreType.DMA((2,)),
         ],
         compiler_params=pltpu.CompilerParams(
             collective_id=0, has_side_effects=True, vmem_limit_bytes=58 * 2**20

time: 68 us -> 61.2 us (0.900); the launches traced: 66.9 us -> 61.1 us
  Pallas kernels: 64 us -> 58.2 us
    pallas_call x1, Pallas kernels: 64 us -> 58.2 us  [local(): pl.pallas_call(functools.partial(kernel, (groups, ranks)), out_shape=(plt...]
where the time goes in v3:
time: 61.2 us; the launch traced here: 61.1 us
  Pallas kernels  58.2 us (95%)
  local copies, waits for them, and re-layouts  2.2 us (4%)
  between operations  0.64 us (1%)
    pallas_call x1, Pallas kernels, local(): pl.pallas_call(functools.partial(kernel, (groups, ranks)), out_shape=(plt...  58.2 us
    unnamed x3, local copies, waits for them, and re-layouts  2.2 us

profile of v3, /device:TPU:1, one launch (start us, length us, event | category | flops | bytes accessed | tf_op | source)
XLA Modules:
  0.0 61.1 jit_solution(16869508253861120536)
XLA Ops:
  0.6 58.2 %panorama.1 = (bf16[128,16,128]{2,1,0:T(8,128)(2,1)S(1)}, bf16[128,16,128]{2,1,0:T(8,128)(2,1)S(1)}, f32[4,16,36]{2,1,0:T(8,128)S(1)}) custom-call(bf16[128,16,128]{2,1,0:T(8,128)(2,1)} %bitcast.8, bf16[4,9,128,128]{3,2,1,0:T(8,128)(2,1)} %weights_ref.1, bf16[128,16,128]{2,1,0:T(8,128)(2,1)} %bitcast.9), custom_call_target="tpu_custom_call" | custom-call | tf_op jit(solution)/shard_map/panorama/pallas_call | solution.py:390
  58.9 0.8 %copy.9 = bf16[1,128,16,128]{3,2,1,0:T(8,128)(2,1)} copy(bf16[1,128,16,128]{3,2,1,0:T(8,128)(2,1)S(1)} %bitcast.6) | data formatting | bytes 1048576
  59.7 0.8 %copy.10 = bf16[1,128,16,128]{3,2,1,0:T(8,128)(2,1)} copy(bf16[1,128,16,128]{3,2,1,0:T(8,128)(2,1)S(1)} %bitcast.5) | data formatting | bytes 1048576
  60.4 0.6 %copy.11 = f32[4,36,16]{1,2,0:T(8,128)} copy(f32[4,36,16]{1,2,0:T(8,128)S(1)} %bitcast.7) | data formatting | bytes 18432

commit v4 on v3

--- a/solution.py
+++ b/solution.py
@@ -18,7 +18,7 @@
 SIGNAL_PAD = (1, 2, 6, 8)
 SLOPE_PAD = (0, 2, 0)
 PIECES = (
-    (((0, 1), (1, 2), (3, 2), (5, 2)), ((15, 1), (13, 2), (11, 2), (9, 2))),
+    (((0, 3), (3, 4)), ((13, 3), (9, 4))),
     (((0, 2), (4, 2), (2, 2), (6, 2)), ((8, 2), (12, 2), (10, 2), (14, 2))),
     (((0, 2), (4, 2), (2, 2), (6, 2)), ((8, 2), (12, 2), (10, 2), (14, 2))),
     (((0, 2), (4, 2), (2, 2)), ((12, 2), (10, 2), (14, 2))),
@@ -38,8 +38,8 @@
     levels = scratch[8:12]
     signals = scratch[12:16]
     slopes = scratch[16:19]
-    send_b, recv_b, send_l, recv_l, local_sem = scratch[19:24]
-    halo_send, halo_recv, batch_send, batch_recv, lon_send, lon_recv = scratch[24:30]
+    send_b, recv_b, send_l, recv_l, partial, local_sem = scratch[19:25]
+    halo_send, halo_recv, batch_send, batch_recv, lon_send, lon_recv = scratch[25:31]
 
     lon = lax.axis_index("lon")
     batch = lax.axis_index("batch")
@@ -129,23 +129,46 @@
                         pl.ds((3 * span + row) * channels, channels),
                     ] = tap_block(number, row, span - side, True)
 
-    def gathered(buffer, pad, dilation, column, spans=4):
+    def gathered(buffer, pad, dilation, column, spans=range(4)):
         return jnp.concatenate(
             [
                 buffer[row, pad + column + (span - 1) * dilation]
-                for span in range(spans)
+                for span in spans
                 for row in range(3)
             ],
             axis=-1,
         )
 
+    inner, outer = (1, 2), (0, 3)
+    third = 3 * channels
+
+    def forward_part(number, column, spans):
+        return jnp.dot(
+            gathered(levels[number], LEVEL_PAD[number], 2**number, column, spans),
+            jnp.concatenate([forward_w[number, pl.ds(span * third, third), :] for span in spans], axis=0),
+            preferred_element_type=F32,
+        )
+
+    def backward_part(number, column, spans, sides=2):
+        return lax.dot_general(
+            gathered(signals[number], SIGNAL_PAD[number], 2**number, column, spans),
+            jnp.concatenate(
+                [
+                    backward_w[number, pl.ds(0, sides * channels), pl.ds(span * third, third)]
+                    for span in spans
+                ],
+                axis=1,
+            ),
+            (((1,), (1,)), ((), ())),
+            preferred_element_type=F32,
+        )
+
     def forward_pair(number, column):
         dilation = 2**number
-        summed = jnp.dot(
-            gathered(levels[number], LEVEL_PAD[number], dilation, column),
-            forward_w[number],
-            preferred_element_type=F32,
-        )
+        if number + 1 < LAYERS:
+            summed = forward_part(number, column, range(4))
+        else:
+            summed = partial[column] + forward_part(number, column, outer)
         for side in range(2):
             here = column + side * dilation
             z = summed[:, side * channels : (side + 1) * channels]
@@ -166,13 +189,10 @@
 
     def backward_columns(number, column, sides):
         dilation = 2**number
-        spans = 2 + sides
-        back = lax.dot_general(
-            gathered(signals[number], SIGNAL_PAD[number], dilation, column, spans),
-            backward_w[number, pl.ds(0, sides * channels), pl.ds(0, 3 * spans * channels)],
-            (((1,), (1,)), ((), ())),
-            preferred_element_type=F32,
-        )
+        if number + 1 < LAYERS:
+            back = backward_part(number, column, range(2 + sides), sides)
+        else:
+            back = partial[column] + backward_part(number, column, outer)
         for side in range(sides):
             here = column + side * dilation
             value = back[:, side * channels : (side + 1) * channels]
@@ -277,7 +297,7 @@
     level, pad = levels[0], LEVEL_PAD[0]
     level[1, pad : pad + width] = swapped(staged[...])
     pl.semaphore_wait(barrier, groups + ranks - 2)
-    for piece in range(4):
+    for piece in range(2):
         for side in range(2):
             halo_copy(0, side, piece).start()
     edge_rows = jnp.zeros((PAD, channels), F32)
@@ -297,44 +317,47 @@
     columns_up[...] = swapped(upstream[...])
     for number in (2, 3):
         build_forward(number)
+    for number in range(LAYERS):
+        build_backward(number)
     for half in range(2):
-        for piece in (2 * half, 2 * half + 1):
-            receive(0, 0, piece, 1)
-            receive(0, 1, piece, 1)
-        for piece in (2 * half, 2 * half + 1):
-            forward_pair(0, -2 * piece)
-            forward_pair(0, width - 2 + 2 * piece)
+        receive(0, 0, half, 1)
+        receive(0, 1, half, 1)
+        for place in (2 * half, 2 * half + 1):
+            forward_pair(0, -2 * place)
+            forward_pair(0, width - 2 + 2 * place)
         for column in ((0, 1, 12, 13), (-4, -3, 16, 17))[half]:
             forward_pair(1, column)
-    for first in (0, 2):
-        for side in range(2):
-            for column in (first, first + 1):
-                forward_pair(2, column + 8 * side)
-            halo_copy(1, side, first).start()
-            halo_copy(1, side, first + 1).start()
-    for number in range(LAYERS):
-        build_backward(number)
-    for half, columns in enumerate(((0, 1, 4, 5), (2, 3, 6, 7))):
+    halves = ((0, 1, 4, 5), (2, 3, 6, 7))
+    for half in range(2):
+        for column in (0, 8, 1, 9) if half == 0 else (2, 10, 3, 11):
+            forward_pair(2, column)
+        for piece in (2 * half, 2 * half + 1):
+            for side in range(2):
+                halo_copy(1, side, piece).start()
+    for column in range(8):
+        partial[column] = forward_part(3, column, inner)
+    for half in range(2):
         for piece in (2 * half, 2 * half + 1):
             receive(1, 0, piece, 8)
             receive(1, 1, piece, 8)
-        for place, column in enumerate(columns):
+        for column in halves[half]:
             forward_pair(3, column)
-            if place % 2:
-                halo_copy(2, 0, 2 * half + place // 2).start()
-                halo_copy(2, 1, 2 * half + place // 2).start()
-
+        for piece in (2 * half, 2 * half + 1):
+            for side in range(2):
+                halo_copy(2, side, piece).start()
+
+    for column in range(8):
+        partial[column] = backward_part(3, column, inner)
     features_ref[...] = swapped(slabs[...])
-    ready = (((0, 0),), ((0, 1), (1, 0)), ((0, 2), (1, 1)), ((1, 2),))
-    for half, columns in enumerate(((0, 1, 4, 5), (2, 3, 6, 7))):
+    ready = (((0, 0), (0, 1), (1, 0)), ((0, 2), (1, 1), (1, 2)))
+    for half in range(2):
         for piece in (2 * half, 2 * half + 1):
             receive(2, 0, piece, 8)
             receive(2, 1, piece, 8)
-        for place, column in enumerate(columns):
+        for column in halves[half]:
             backward_columns(3, column, 2)
-            if place % 2:
-                for side, part in ready[2 * half + place // 2]:
-                    halo_copy(3, side, part).start()
+        for side, part in ready[half]:
+            halo_copy(3, side, part).start()
     weight_grad(3)
     start_batch(3)
     weight_grad(2)
@@ -362,9 +385,6 @@
         backward_columns(0, column, 2)
     input_grad_ref[...] = swapped(slabs[...])
     start_lon(1)
-    finish(0)
-    finish(1)
-
     for which in range(len(PIECES)):
         for side in range(2):
             for piece in range(len(PIECES[which][side])):
@@ -372,9 +392,21 @@
     for number in range(LAYERS):
         sent = send_b.at[number, 1:]
         pltpu.make_async_copy(sent, sent, batch_send.at[number]).wait()
+    finish(0)
+    finish(1)
     for which in range(2):
         sent = send_l.at[which, 1:]
         pltpu.make_async_copy(sent, sent, lon_send.at[which]).wait()
+
+
+def store(*refs):
+    copies = [
+        pltpu.make_async_copy(refs[n], refs[3 + n], refs[6].at[n]) for n in range(3)
+    ]
+    for copy in copies:
+        copy.start()
+    for copy in copies:
+        copy.wait()
 
 
 def local(images, weights, cotangent):
@@ -412,6 +444,7 @@
             pltpu.VMEM((LAYERS, ranks, 9 * block, channels), BF16),
             pltpu.VMEM((2, groups, block, channels), BF16),
             pltpu.VMEM((2, groups, block, channels), BF16),
+            pltpu.VMEM((width // 2, rows, 2 * channels), F32),
             pltpu.SemaphoreType.DMA((3,)),
             pltpu.SemaphoreType.DMA((len(PIECES), 2, 4)),
             pltpu.SemaphoreType.DMA((len(PIECES), 2, 4)),
@@ -425,6 +458,18 @@
         ),
         name="panorama",
     )(images.reshape(field), weights, cotangent.reshape(field))
+    features, input_grad, owned = pl.pallas_call(
+        store,
+        out_shape=(
+            jax.ShapeDtypeStruct(field, BF16),
+            jax.ShapeDtypeStruct(field, BF16),
+            jax.ShapeDtypeStruct((LAYERS, block, share), F32),
+        ),
+        in_specs=[pl.BlockSpec(memory_space=pltpu.VMEM)] * 3,
+        out_specs=[pl.BlockSpec(memory_space=pl.ANY)] * 3,
+        scratch_shapes=[pltpu.SemaphoreType.DMA((3,))],
+        name="store",
+    )(*[pltpu.with_memory_space_constraint(x, pltpu.VMEM) for x in (features, input_grad, owned)])
     weight_grads = jnp.swapaxes(owned, 1, 2)
     return features.reshape(images.shape), input_grad.reshape(images.shape), weight_grads
 

time: 61.2 us -> 59.8 us (0.977)
  local copies, waits for them, and re-layouts: 2.2 us -> 0 us
  Pallas kernels: 58.2 us -> 58.9 us
    unnamed x3 -> x0, local copies, waits for them, and re-layouts: 2.2 us -> none
    pallas_call x0 -> x1, Pallas kernels: none -> 1 us  [local(): pl.pallas_call(store, out_shape=(jax.ShapeDtypeStruct(field, BF16), jax.S...]
where the time goes in v4:
time: 59.8 us; the launch traced here: 59.7 us
  Pallas kernels  58.9 us (98%)
  between operations  0.8 us (1%)
    pallas_call x1, Pallas kernels, local(): pl.pallas_call(functools.partial(kernel, (groups, ranks)), out_shape=(plt...  57.9 us

profile of v4, /device:TPU:1, one launch (start us, length us, event | category | flops | bytes accessed | tf_op | source)
XLA Modules:
  0.0 59.7 jit_solution(5499258839008581561)
XLA Ops:
  0.6 57.9 %panorama.1 = (bf16[128,16,128]{2,1,0:T(8,128)(2,1)S(1)}, bf16[128,16,128]{2,1,0:T(8,128)(2,1)S(1)}, f32[4,16,36]{2,1,0:T(8,128)S(1)}) custom-call(bf16[128,16,128]{2,1,0:T(8,128)(2,1)} %bitcast.5, bf16[4,9,128,128]{3,2,1,0:T(8,128)(2,1)} %weights_ref.1, bf16[128,16,128]{2,1,0:T(8,128)(2,1)} %bitcast.6), custom_call_target="tpu_custom_call" | custom-call | tf_op jit(solution)/shard_map/panorama/pallas_call | solution.py:422
  58.6 1.0 %store.1 = (bf16[128,16,128]{2,1,0:T(8,128)(2,1)}, bf16[128,16,128]{2,1,0:T(8,128)(2,1)}, f32[4,16,36]{2,1,0:T(8,128)}) custom-call(bf16[128,16,128]{2,1,0:T(8,128)(2,1)S(1)} %get-tuple-element.9.refs_0_, bf16[128,16,128]{2,1,0:T(8,128)(2,1)S(1)} %get-tuple-element.10.refs_1_, f32[4,16,36]{2,1,0:T(8,128)S(1)} %get-tuple-element.11.refs_2_), custom_call_target="tpu_custom_call" | custom-call | tf_op jit(solution)/shard_map/store/pallas_call | solution.py:461

commit v5 on v4

--- a/solution.py
+++ b/solution.py
@@ -39,7 +39,7 @@
     signals = scratch[12:16]
     slopes = scratch[16:19]
     send_b, recv_b, send_l, recv_l, partial, local_sem = scratch[19:25]
-    halo_send, halo_recv, batch_send, batch_recv, lon_send, lon_recv = scratch[25:31]
+    halo_send, halo_recv, batch_send, batch_recv, lon_send, lon_recv, known = scratch[25:32]
 
     lon = lax.axis_index("lon")
     batch = lax.axis_index("batch")
@@ -48,26 +48,32 @@
     block = channels // ranks
     share = 9 * channels // groups
 
+    barrier = pltpu.get_barrier_semaphore()
+    axes = (("lon", lon, groups), ("batch", batch, ranks))
+
+    def tell(semaphore, which, apart):
+        name, here, size = axes[which]
+        for peer in (lax.rem(here + apart, size), lax.rem(here + size - apart, size)):
+            pl.semaphore_signal(semaphore, inc=1, device_id={name: peer}, device_id_type=MESH)
+
+    def tell_round(turn):
+        for which, (_, _, size) in enumerate(axes):
+            if 4 * 2**turn <= size:
+                tell(known.at[which, turn], which, 2**turn)
+
+    def hear_round(turn):
+        for which, (_, _, size) in enumerate(axes):
+            if 4 * 2**turn <= size:
+                pl.semaphore_wait(known.at[which, turn], 2)
+
     fetch_images = pltpu.make_async_copy(images_ref, staged, local_sem.at[0])
     fetch_taps = pltpu.make_async_copy(weights_ref, taps, local_sem.at[1])
     fetch_upstream = pltpu.make_async_copy(cotangent_ref, upstream, local_sem.at[2])
     fetch_images.start()
+    tell(barrier, 0, 1)
+    tell(barrier, 1, 1)
     fetch_taps.start()
     fetch_upstream.start()
-
-    barrier = pltpu.get_barrier_semaphore()
-
-    @pl.loop(1, groups)
-    def _(step):
-        pl.semaphore_signal(
-            barrier, inc=1, device_id={"lon": lax.rem(lon + step, groups)}, device_id_type=MESH
-        )
-
-    @pl.loop(1, ranks)
-    def _(step):
-        pl.semaphore_signal(
-            barrier, inc=1, device_id={"batch": lax.rem(batch + step, ranks)}, device_id_type=MESH
-        )
 
     exchanged = (
         (levels[0], LEVEL_PAD[0]),
@@ -204,7 +210,7 @@
             else:
                 slabs[here] = value.astype(BF16)
 
-    def weight_grad(number):
+    def weight_grad(number, cut=None):
         dilation = 2**number
         pad, level_pad = SIGNAL_PAD[number], LEVEL_PAD[number]
         signal = signals[number][1, pad : pad + width].reshape(rows * width, channels)
@@ -221,17 +227,20 @@
                 signal, taken, (((0,), (0,)), ((), ())), preferred_element_type=F32
             ).astype(BF16)
             for i in range(3):
-                send_b[number, :, pl.ds((3 * i + j) * block, block), :] = total[
+                send_b[number, :, pl.ds((3 * j + i) * block, block), :] = total[
                     :, i * channels : (i + 1) * channels
                 ].reshape(ranks, block, channels)
-
-    def start_batch(number):
+            if cut is not None and j + 1 == cut:
+                start_batch(number, 0, cut)
+        start_batch(number, cut or 0, 3)
+
+    def start_batch(number, first, last):
         half = ranks // 4
         for step in (half, 3 * half, *(n for n in range(1, ranks) if n not in (half, 3 * half))):
             target = lax.rem(batch + step, ranks)
             pltpu.make_async_remote_copy(
-                src_ref=send_b.at[number, target],
-                dst_ref=recv_b.at[number, step],
+                src_ref=send_b.at[number, target, pl.ds(3 * first * block, 3 * (last - first) * block)],
+                dst_ref=recv_b.at[number, step, pl.ds(3 * first * block, 3 * (last - first) * block)],
                 send_sem=batch_send.at[number],
                 recv_sem=batch_recv.at[number],
                 device_id={"batch": target},
@@ -253,7 +262,8 @@
             totals.append(total)
 
         def shifted(total, tap, amount):
-            value = total[tap * block : (tap + 1) * block]
+            place = 3 * (tap % 3) + tap // 3
+            value = total[place * block : (place + 1) * block]
             return pltpu.roll(value, amount, 1) if amount else value
 
         for target in range(groups):
@@ -296,10 +306,11 @@
     fetch_images.wait()
     level, pad = levels[0], LEVEL_PAD[0]
     level[1, pad : pad + width] = swapped(staged[...])
-    pl.semaphore_wait(barrier, groups + ranks - 2)
+    pl.semaphore_wait(barrier, 4)
     for piece in range(2):
         for side in range(2):
             halo_copy(0, side, piece).start()
+    tell_round(0)
     edge_rows = jnp.zeros((PAD, channels), F32)
     for slot in range(shifter.shape[0]):
         shifter[slot, pl.ds(0, PAD), :] = edge_rows
@@ -319,6 +330,8 @@
         build_forward(number)
     for number in range(LAYERS):
         build_backward(number)
+    hear_round(0)
+    tell_round(1)
     for half in range(2):
         receive(0, 0, half, 1)
         receive(0, 1, half, 1)
@@ -336,6 +349,8 @@
                 halo_copy(1, side, piece).start()
     for column in range(8):
         partial[column] = forward_part(3, column, inner)
+    hear_round(1)
+    tell_round(2)
     for half in range(2):
         for piece in (2 * half, 2 * half + 1):
             receive(1, 0, piece, 8)
@@ -350,6 +365,8 @@
         partial[column] = backward_part(3, column, inner)
     features_ref[...] = swapped(slabs[...])
     ready = (((0, 0), (0, 1), (1, 0)), ((0, 2), (1, 1), (1, 2)))
+    hear_round(2)
+    tell_round(3)
     for half in range(2):
         for piece in (2 * half, 2 * half + 1):
             receive(2, 0, piece, 8)
@@ -359,9 +376,7 @@
         for side, part in ready[half]:
             halo_copy(3, side, part).start()
     weight_grad(3)
-    start_batch(3)
     weight_grad(2)
-    start_batch(2)
     for side in range(2):
         for piece in range(3):
             receive(3, side, piece, 4)
@@ -375,16 +390,16 @@
             halo_copy(4, 0, 0).start()
             halo_copy(4, 1, 0).start()
     weight_grad(0)
-    start_batch(0)
-    weight_grad(1)
-    start_batch(1)
+    weight_grad(1, 2)
+    hear_round(3)
     start_lon(0)
+    start_lon(1)
     receive(4, 0, 0, 1)
     receive(4, 1, 0, 1)
     for column in range(0, width, 2):
         backward_columns(0, column, 2)
     input_grad_ref[...] = swapped(slabs[...])
-    start_lon(1)
+
     for which in range(len(PIECES)):
         for side in range(2):
             for piece in range(len(PIECES[which][side])):
@@ -452,6 +467,7 @@
             pltpu.SemaphoreType.DMA((LAYERS,)),
             pltpu.SemaphoreType.DMA((2,)),
             pltpu.SemaphoreType.DMA((2,)),
+            pltpu.SemaphoreType.REGULAR((2, 4)),
         ],
         compiler_params=pltpu.CompilerParams(
             collective_id=0, has_side_effects=True, vmem_limit_bytes=58 * 2**20

time: 59.8 us -> 57.9 us (0.968)
  Pallas kernels: 58.9 us -> 57 us
    pallas_call x1, Pallas kernels: 57.9 us -> 56 us  [local(): pl.pallas_call(functools.partial(kernel, (groups, ranks)), out_shape=(plt...]
where the time goes in v5:
time: 57.9 us; the launch traced here: 57.8 us
  Pallas kernels  57 us (98%)
  between operations  0.8 us (1%)
    pallas_call x1, Pallas kernels, local(): pl.pallas_call(functools.partial(kernel, (groups, ranks)), out_shape=(plt...  56 us

profile of v5, /device:TPU:1, one launch (start us, length us, event | category | flops | bytes accessed | tf_op | source)
XLA Modules:
  0.0 57.8 jit_solution(7642994788865008146)
XLA Ops:
  0.6 56.0 %panorama.1 = (bf16[128,16,128]{2,1,0:T(8,128)(2,1)S(1)}, bf16[128,16,128]{2,1,0:T(8,128)(2,1)S(1)}, f32[4,16,36]{2,1,0:T(8,128)S(1)}) custom-call(bf16[128,16,128]{2,1,0:T(8,128)(2,1)} %bitcast.5, bf16[4,9,128,128]{3,2,1,0:T(8,128)(2,1)} %weights_ref.1, bf16[128,16,128]{2,1,0:T(8,128)(2,1)} %bitcast.6), custom_call_target="tpu_custom_call" | custom-call | tf_op jit(solution)/shard_map/panorama/pallas_call | solution.py:437
  56.7 1.0 %store.1 = (bf16[128,16,128]{2,1,0:T(8,128)(2,1)}, bf16[128,16,128]{2,1,0:T(8,128)(2,1)}, f32[4,16,36]{2,1,0:T(8,128)}) custom-call(bf16[128,16,128]{2,1,0:T(8,128)(2,1)S(1)} %get-tuple-element.9.refs_0_, bf16[128,16,128]{2,1,0:T(8,128)(2,1)S(1)} %get-tuple-element.10.refs_1_, f32[4,16,36]{2,1,0:T(8,128)S(1)} %get-tuple-element.11.refs_2_), custom_call_target="tpu_custom_call" | custom-call | tf_op jit(solution)/shard_map/store/pallas_call | solution.py:477

commit v6 on v5

--- a/solution.py
+++ b/solution.py
@@ -195,7 +195,10 @@
 
     def backward_columns(number, column, sides):
         dilation = 2**number
-        if number + 1 < LAYERS:
+        if number == 2 and sides == 2:
+            outside = (0,) if column < dilation else (3,)
+            back = partial[column % 8 + column // 8 * 4] + backward_part(number, column, outside)
+        elif number + 1 < LAYERS:
             back = backward_part(number, column, range(2 + sides), sides)
         else:
             back = partial[column] + backward_part(number, column, outer)
@@ -340,43 +343,44 @@
             forward_pair(0, width - 2 + 2 * place)
         for column in ((0, 1, 12, 13), (-4, -3, 16, 17))[half]:
             forward_pair(1, column)
-    halves = ((0, 1, 4, 5), (2, 3, 6, 7))
+    firsts = (0, 4, 2, 6)
     for half in range(2):
-        for column in (0, 8, 1, 9) if half == 0 else (2, 10, 3, 11):
-            forward_pair(2, column)
-        for piece in (2 * half, 2 * half + 1):
-            for side in range(2):
+        for side in range(2):
+            for column in (2 * half, 2 * half + 1):
+                forward_pair(2, column + 8 * side)
+            for piece in (2 * half, 2 * half + 1):
                 halo_copy(1, side, piece).start()
     for column in range(8):
         partial[column] = forward_part(3, column, inner)
     hear_round(1)
     tell_round(2)
-    for half in range(2):
-        for piece in (2 * half, 2 * half + 1):
-            receive(1, 0, piece, 8)
-            receive(1, 1, piece, 8)
-        for column in halves[half]:
+    for piece, first in enumerate(firsts):
+        for side in range(2):
+            receive(1, side, piece, 8)
+        for column in (first, first + 1):
             forward_pair(3, column)
-        for piece in (2 * half, 2 * half + 1):
-            for side in range(2):
-                halo_copy(2, side, piece).start()
+        for side in range(2):
+            halo_copy(2, side, piece).start()
 
     for column in range(8):
         partial[column] = backward_part(3, column, inner)
     features_ref[...] = swapped(slabs[...])
-    ready = (((0, 0), (0, 1), (1, 0)), ((0, 2), (1, 1), (1, 2)))
+    ready = (((0, 0),), ((0, 1), (1, 0)), ((0, 2), (1, 1)), ((1, 2),))
     hear_round(2)
     tell_round(3)
-    for half in range(2):
-        for piece in (2 * half, 2 * half + 1):
-            receive(2, 0, piece, 8)
-            receive(2, 1, piece, 8)
-        for column in halves[half]:
+    for piece, first in enumerate(firsts):
+        for side in range(2):
+            receive(2, side, piece, 8)
+        for column in (first, first + 1):
             backward_columns(3, column, 2)
-        for side, part in ready[half]:
+        for side, part in ready[piece]:
             halo_copy(3, side, part).start()
     weight_grad(3)
     weight_grad(2)
+    for column in (0, 1, 2, 3, 8, 9, 10, 11):
+        partial[column % 8 + column // 8 * 4] = backward_part(
+            2, column, (1, 2, 3) if column < 4 else (0, 1, 2)
+        )
     for side in range(2):
         for piece in range(3):
             receive(3, side, piece, 4)

time: 57.9 us -> 55.3 us (0.955)
  Pallas kernels: 57 us -> 54.4 us
    pallas_call x1, Pallas kernels: 56 us -> 53.4 us  [local(): pl.pallas_call(functools.partial(kernel, (groups, ranks)), out_shape=(plt...]
where the time goes in v6:
time: 55.3 us; the launch traced here: 55.2 us
  Pallas kernels  54.4 us (98%)
  between operations  0.8 us (1%)
    pallas_call x1, Pallas kernels, local(): pl.pallas_call(functools.partial(kernel, (groups, ranks)), out_shape=(plt...  53.4 us

profile of v6, /device:TPU:1, one launch (start us, length us, event | category | flops | bytes accessed | tf_op | source)
XLA Modules:
  0.0 55.2 jit_solution(16876221112627480941)
XLA Ops:
  0.6 53.4 %panorama.1 = (bf16[128,16,128]{2,1,0:T(8,128)(2,1)S(1)}, bf16[128,16,128]{2,1,0:T(8,128)(2,1)S(1)}, f32[4,16,36]{2,1,0:T(8,128)S(1)}) custom-call(bf16[128,16,128]{2,1,0:T(8,128)(2,1)} %bitcast.5, bf16[4,9,128,128]{3,2,1,0:T(8,128)(2,1)} %weights_ref.1, bf16[128,16,128]{2,1,0:T(8,128)(2,1)} %bitcast.6), custom_call_target="tpu_custom_call" | custom-call | tf_op jit(solution)/shard_map/panorama/pallas_call | solution.py:441
  54.1 1.0 %store.1 = (bf16[128,16,128]{2,1,0:T(8,128)(2,1)}, bf16[128,16,128]{2,1,0:T(8,128)(2,1)}, f32[4,16,36]{2,1,0:T(8,128)}) custom-call(bf16[128,16,128]{2,1,0:T(8,128)(2,1)S(1)} %get-tuple-element.9.refs_0_, bf16[128,16,128]{2,1,0:T(8,128)(2,1)S(1)} %get-tuple-element.10.refs_1_, f32[4,16,36]{2,1,0:T(8,128)S(1)} %get-tuple-element.11.refs_2_), custom_call_target="tpu_custom_call" | custom-call | tf_op jit(solution)/shard_map/store/pallas_call | solution.py:481

commit v7 on v6

--- a/solution.py
+++ b/solution.py
@@ -19,8 +19,8 @@
 SLOPE_PAD = (0, 2, 0)
 PIECES = (
     (((0, 3), (3, 4)), ((13, 3), (9, 4))),
-    (((0, 2), (4, 2), (2, 2), (6, 2)), ((8, 2), (12, 2), (10, 2), (14, 2))),
-    (((0, 2), (4, 2), (2, 2), (6, 2)), ((8, 2), (12, 2), (10, 2), (14, 2))),
+    (tuple((c, 1) for c in range(8)), tuple((c, 1) for c in range(8, 16))),
+    (tuple((c, 1) for c in range(8)), tuple((c, 1) for c in range(8, 16))),
     (((0, 2), (4, 2), (2, 2)), ((12, 2), (10, 2), (14, 2))),
     (((0, 1),), ((15, 1),)),
 )
@@ -343,24 +343,23 @@
             forward_pair(0, width - 2 + 2 * place)
         for column in ((0, 1, 12, 13), (-4, -3, 16, 17))[half]:
             forward_pair(1, column)
-    firsts = (0, 4, 2, 6)
+    order = (0, 1, 4, 5, 2, 3, 6, 7)
     for half in range(2):
         for side in range(2):
             for column in (2 * half, 2 * half + 1):
                 forward_pair(2, column + 8 * side)
-            for piece in (2 * half, 2 * half + 1):
+            for piece in (2 * half, 2 * half + 1, 2 * half + 4, 2 * half + 5):
                 halo_copy(1, side, piece).start()
     for column in range(8):
         partial[column] = forward_part(3, column, inner)
     hear_round(1)
     tell_round(2)
-    for piece, first in enumerate(firsts):
-        for side in range(2):
-            receive(1, side, piece, 8)
-        for column in (first, first + 1):
-            forward_pair(3, column)
-        for side in range(2):
-            halo_copy(2, side, piece).start()
+    for column in order:
+        for side in range(2):
+            receive(1, side, column, 8)
+        forward_pair(3, column)
+        for side in range(2):
+            halo_copy(2, side, column).start()
 
     for column in range(8):
         partial[column] = backward_part(3, column, inner)
@@ -368,12 +367,11 @@
     ready = (((0, 0),), ((0, 1), (1, 0)), ((0, 2), (1, 1)), ((1, 2),))
     hear_round(2)
     tell_round(3)
-    for piece, first in enumerate(firsts):
-        for side in range(2):
-            receive(2, side, piece, 8)
-        for column in (first, first + 1):
-            backward_columns(3, column, 2)
-        for side, part in ready[piece]:
+    for place, column in enumerate(order):
+        for side in range(2):
+            receive(2, side, column, 8)
+        backward_columns(3, column, 2)
+        for side, part in ready[place // 2] if place % 2 else ():
             halo_copy(3, side, part).start()
     weight_grad(3)
     weight_grad(2)
@@ -465,8 +463,8 @@
             pltpu.VMEM((2, groups, block, channels), BF16),
             pltpu.VMEM((width // 2, rows, 2 * channels), F32),
             pltpu.SemaphoreType.DMA((3,)),
-            pltpu.SemaphoreType.DMA((len(PIECES), 2, 4)),
-            pltpu.SemaphoreType.DMA((len(PIECES), 2, 4)),
+            pltpu.SemaphoreType.DMA((len(PIECES), 2, 8)),
+            pltpu.SemaphoreType.DMA((len(PIECES), 2, 8)),
             pltpu.SemaphoreType.DMA((LAYERS,)),
             pltpu.SemaphoreType.DMA((LAYERS,)),
             pltpu.SemaphoreType.DMA((2,)),

time: 55.3 us -> 55.9 us (1.011)
  Pallas kernels: 54.4 us -> 55 us
where the time goes in v7:
time: 55.9 us; the launch traced here: 55.8 us
  Pallas kernels  55 us (98%)
  between operations  0.8 us (1%)
    pallas_call x1, Pallas kernels, local(): pl.pallas_call(functools.partial(kernel, (groups, ranks)), out_shape=(plt...  54 us

profile of v7, /device:TPU:1, one launch (start us, length us, event | category | flops | bytes accessed | tf_op | source)
XLA Modules:
  0.0 55.8 jit_solution(7806541679534691560)
XLA Ops:
  0.6 54.0 %panorama.1 = (bf16[128,16,128]{2,1,0:T(8,128)(2,1)S(1)}, bf16[128,16,128]{2,1,0:T(8,128)(2,1)S(1)}, f32[4,16,36]{2,1,0:T(8,128)S(1)}) custom-call(bf16[128,16,128]{2,1,0:T(8,128)(2,1)} %bitcast.5, bf16[4,9,128,128]{3,2,1,0:T(8,128)(2,1)} %weights_ref.1, bf16[128,16,128]{2,1,0:T(8,128)(2,1)} %bitcast.6), custom_call_target="tpu_custom_call" | custom-call | tf_op jit(solution)/shard_map/panorama/pallas_call | solution.py:439
  54.6 1.0 %store.1 = (bf16[128,16,128]{2,1,0:T(8,128)(2,1)}, bf16[128,16,128]{2,1,0:T(8,128)(2,1)}, f32[4,16,36]{2,1,0:T(8,128)}) custom-call(bf16[128,16,128]{2,1,0:T(8,128)(2,1)S(1)} %get-tuple-element.9.refs_0_, bf16[128,16,128]{2,1,0:T(8,128)(2,1)S(1)} %get-tuple-element.10.refs_1_, f32[4,16,36]{2,1,0:T(8,128)S(1)} %get-tuple-element.11.refs_2_), custom_call_target="tpu_custom_call" | custom-call | tf_op jit(solution)/shard_map/store/pallas_call | solution.py:479
